TPU v7x, 256 devices: a whole 4x4x8 slice. The times are simulated.
256 devices in a mesh: seq: 64 (over x, y_lo, z), chan: 4 (over y_hi, core).
Axes of the slice: x: 4, y: 4 (y_hi: 2, y_lo: 2; y = y_hi * 2 + y_lo), z: 8, core: 2. Of those that a mesh axis runs over, the one named last changes fastest.
Arguments:
- q_stream: bfloat16 [8192, 2048], P('seq', 'chan'), may hold values from -6 to 6
- k_stream: bfloat16 [8192, 2048], P('seq', 'chan'), may hold values from -6 to 6
- v_stream: bfloat16 [8192, 2048], P('seq', 'chan'), may hold values from -6 to 6
- short_taps: float32 [3, 3, 2048], P(None, None, 'chan'), may hold values from -3.5 to 3.5
- long_filter: float32 [8192, 2048], P('seq', 'chan'), may hold values from -2 to 2
- skip_gain: float32 [2048], P('chan'), may hold values from -6 to 6
- out_weight: bfloat16 [2048, 4096], P('chan'), may hold values from -0.1875 to 0.1875
Outputs:
- mixed_out: bfloat16 [8192, 4096], P('seq', 'chan')
All inputs are finite; a program needn't handle non-finite values.
Results may differ from a plain program's by a relative error of at most 0.0095.
Values may be sent and summed in bfloat16 or wider, within the bound.
A program may use at most 64 MiB of HBM per device.

v0:
```python
import math

import jax
import jax.numpy as jnp
from jax import lax
from jax.sharding import PartitionSpec as P


def from_partner(x, axis, apart):
    return lax.ppermute(x, axis, [(i, i ^ 1 << apart) for i in range(lax.axis_size(axis))])


def shifted(block, axis, distance):
    devices = range(lax.axis_size(axis))
    route = [(i - distance, i) for i in devices if i - distance in devices]
    return lax.ppermute(block, axis, route)


def complex_mix(matrix_real, matrix_imag, operand, pattern):
    best = lax.Precision.HIGHEST
    real_part = jnp.einsum(pattern, matrix_real, operand[0], precision=best) - jnp.einsum(
        pattern, matrix_imag, operand[1], precision=best
    )
    imag_part = jnp.einsum(pattern, matrix_real, operand[1], precision=best) + jnp.einsum(
        pattern, matrix_imag, operand[0], precision=best
    )
    return jnp.stack([real_part, imag_part])


def rotate(operand, angles):
    cosine = jnp.cos(angles)
    sine_part = jnp.sin(angles)
    return jnp.stack(
        [operand[0] * cosine - operand[1] * sine_part, operand[0] * sine_part + operand[1] * cosine]
    )


def reversed_bits(bit_source, levels):
    reversed_value = jnp.zeros((), jnp.int32)
    for bit_level in range(levels):
        reversed_value = reversed_value + (bit_source >> bit_level & 1) * (
            1 << levels - 1 - bit_level
        )
    return reversed_value


def pair_forward(signal_data, position, levels):
    for bit_level in reversed(range(levels)):
        half_span = 1 << bit_level
        partner = from_partner(signal_data, "seq", bit_level)
        upper_bit = position >> bit_level & 1
        offset = (position & half_span - 1).astype(jnp.float32)
        turned = rotate(partner - signal_data, -math.pi * offset / half_span)
        signal_data = jnp.where(upper_bit == 1, turned, signal_data + partner)
    return signal_data


def pair_inverse(signal_data, position, levels):
    for bit_level in range(levels):
        half_span = 1 << bit_level
        partner = from_partner(signal_data, "seq", bit_level)
        upper_bit = position >> bit_level & 1
        offset = (position & half_span - 1).astype(jnp.float32)
        angles = math.pi * offset / half_span
        signal_data = jnp.where(
            upper_bit == 1,
            partner - rotate(signal_data, angles),
            signal_data + rotate(partner, angles),
        )
    return signal_data


def body(q_stream, k_stream, v_stream, short_taps, long_filter, skip_gain, out_weight):
    tok_rows = q_stream.shape[0]
    seq_count = lax.axis_size("seq")
    position = lax.axis_index("seq")
    levels = seq_count.bit_length() - 1
    rim_rows = short_taps.shape[1] - 1
    streams = jnp.stack([q_stream, k_stream, v_stream])
    before = shifted(streams[:, tok_rows - rim_rows :], "seq", 1)
    padded = jnp.concatenate([before, streams], axis=1).astype(jnp.float32)
    filtered = jnp.zeros(streams.shape, jnp.float32)
    for lag_index in range(short_taps.shape[1]):
        filtered = (
            filtered
            + short_taps[:, lag_index : lag_index + 1, :]
            * padded[:, rim_rows - lag_index : rim_rows - lag_index + tok_rows]
        )
    q_short = filtered[0]
    product = filtered[1] * filtered[2]
    length = tok_rows * seq_count
    tok_local = jnp.arange(tok_rows, dtype=jnp.int32)
    global_rows = position * tok_rows + tok_local
    phases = -math.pi / length * global_rows.astype(jnp.float32)
    cosine = jnp.cos(phases)[:, None]
    sine_part = jnp.sin(phases)[:, None]
    zero_part = jnp.zeros_like(product)
    real_part = jnp.stack([product, product * cosine, long_filter, long_filter * cosine], axis=1)
    imag_part = jnp.stack(
        [zero_part, product * sine_part, zero_part, long_filter * sine_part], axis=1
    )
    signal_data = jnp.stack([real_part, imag_part])
    signal_data = pair_forward(signal_data, position, levels)
    held_freq = reversed_bits(position, levels)
    twist = -2.0 * math.pi / length * (tok_local * held_freq).astype(jnp.float32)
    signal_data = rotate(signal_data, twist[:, None, None])
    local_angles = (
        2.0
        * math.pi
        / tok_rows
        * (tok_local[:, None] * tok_local[None, :] % tok_rows).astype(jnp.float32)
    )
    local_cos = jnp.cos(local_angles)
    local_sin = jnp.sin(local_angles)
    spectrum = complex_mix(local_cos, -local_sin, signal_data, "kj,jsc->ksc")
    signal_part = spectrum[:, :, 0:2]
    response = spectrum[:, :, 2:4]
    filtered_real = signal_part[0] * response[0] - signal_part[1] * response[1]
    filtered_imag = signal_part[0] * response[1] + signal_part[1] * response[0]
    signal_data = complex_mix(
        local_cos, local_sin, jnp.stack([filtered_real, filtered_imag]), "jk,ksc->jsc"
    )
    signal_data = rotate(signal_data, -twist[:, None, None])
    signal_data = pair_inverse(signal_data, position, levels)
    long_part = (
        signal_data[0][:, 0] + signal_data[0][:, 1] * cosine + signal_data[1][:, 1] * sine_part
    ) / (2.0 * length)
    gated_values = (q_short * (long_part + skip_gain * product)).astype(jnp.bfloat16)
    partial_value = jnp.dot(gated_values, out_weight, preferred_element_type=jnp.float32)
    return lax.psum_scatter(partial_value, "chan", scatter_dimension=1, tiled=True).astype(
        jnp.bfloat16
    )


def solution(mesh):
    in_specs = (
        P("seq", "chan"),
        P("seq", "chan"),
        P("seq", "chan"),
        P(None, None, "chan"),
        P("seq", "chan"),
        P("chan"),
        P("chan", None),
    )
    out_specs = P("seq", "chan")
    return jax.shard_map(body, mesh=mesh, in_specs=in_specs, out_specs=out_specs, check_vma=False)
```

profile of v0, /device:TPU:1, one launch (start us, length us, event | category | flops | bytes accessed | tf_op | source)
XLA Modules:
  0.0 702.1 jit_solution(10311371153296895397)
XLA Ops:
  7.3 4.4 collective-permute-start
  11.8 1.1 multiply_bitcast_fusion.1
  13.7 1.1 maximum_convert_fusion
  16.4 1.6 pad_maximum_fusion
  18.0 6.6 collective-permute-start.1
  24.8 44.5 %collective-permute-done.1 = f32[2,128,4,512]{3,1,2,0:T(8,128)} collective-permute-done((f32[2,128,4,512]{3,1,2,0:T(8,128)}, f32[2,128,4,512]{3,1,2,0:T(8,128)}, u32[]{:S(2)}, u32[]{:S(2)}) %collective-permute-start.1) | collective-permute-done | bytes 2097184 | tf_op jit(solution)/shard_map/ppermute | solution.py:10
  69.3 2.1 fusion.96
  71.7 4.1 maximum_select_fusion
  75.8 1.2 collective-permute-start.2
  77.1 43.9 %collective-permute-done.2 = f32[2,128,4,512]{3,1,2,0:T(8,128)} collective-permute-done((f32[2,128,4,512]{3,1,2,0:T(8,128)}, f32[2,128,4,512]{3,1,2,0:T(8,128)}, u32[]{:S(2)}, u32[]{:S(2)}) %collective-permute-start.2) | collective-permute-done | bytes 2097184 | tf_op jit(solution)/shard_map/ppermute | solution.py:10
  121.1 3.5 fusion.104
  125.8 4.9 maximum_select_fusion.1
  130.9 44.1 %collective-permute-done.3 = f32[2,128,4,512]{3,1,2,0:T(8,128)S(1)} collective-permute-done((f32[2,128,4,512]{3,1,2,0:T(8,128)}, f32[2,128,4,512]{3,1,2,0:T(8,128)S(1)}, u32[]{:S(2)}, u32[]{:S(2)}) %collective-permute-start.3) | collective-permute-done | bytes 2097184 | tf_op jit(solution)/shard_map/ppermute | solution.py:10
  174.9 2.8 sub.129
  178.1 3.0 maximum_select_fusion.2
  181.0 1.6 collective-permute-start.4
  182.9 92.3 %collective-permute-done.4 = f32[2,128,4,512]{3,1,2,0:T(8,128)} collective-permute-done((f32[2,128,4,512]{3,1,2,0:T(8,128)S(1)}, f32[2,128,4,512]{3,1,2,0:T(8,128)}, u32[]{:S(2)}, u32[]{:S(2)}) %collective-permute-start.4) | collective-permute-done | bytes 2097184 | tf_op jit(solution)/shard_map/ppermute | solution.py:10
  275.2 2.1 sub.131
  277.5 3.7 maximum_select_fusion.3
  281.4 91.9 %collective-permute-done.5 = f32[2,128,4,512]{3,1,2,0:T(8,128)S(1)} collective-permute-done((f32[2,128,4,512]{3,1,2,0:T(8,128)}, f32[2,128,4,512]{3,1,2,0:T(8,128)S(1)}, u32[]{:S(2)}, u32[]{:S(2)}) %collective-permute-start.5) | collective-permute-done | bytes 2097184 | tf_op jit(solution)/shard_map/ppermute | solution.py:10
  373.3 2.8 sub.133
  376.5 3.0 maximum_select_fusion.4
  379.8 45.1 %collective-permute-done.6 = f32[2,128,4,512]{3,1,2,0:T(8,128)} collective-permute-done((f32[2,128,4,512]{3,1,2,0:T(8,128)S(1)}, f32[2,128,4,512]{3,1,2,0:T(8,128)}, u32[]{:S(2)}, u32[]{:S(2)}) %collective-permute-start.6) | collective-permute-done | bytes 2097184 | tf_op jit(solution)/shard_map/ppermute | solution.py:10
  424.9 2.1 sub.135
  427.3 2.4 maximum_select_fusion.5
  429.6 1.3 fusion.42
  431.0 1.3 fusion.40
  432.3 1.3 fusion.1
  433.7 1.3 fusion
  437.8 1.0 subtract_bitcast_fusion
  439.4 21.3 %collective-permute-done.7 = f32[2,128,2,512]{3,1,2,0:T(8,128)S(1)} collective-permute-done((f32[2,128,2,512]{3,1,2,0:T(8,128)S(1)}, f32[2,128,2,512]{3,1,2,0:T(8,128)S(1)}, u32[]{:S(2)}, u32[]{:S(2)}) %collective-permute-start.7) | collective-permute-done | bytes 1048608 | tf_op jit(solution)/shard_map/ppermute | solution.py:10
  460.9 1.5 fusion.2
  462.4 5.3 collective-permute-start.8
  468.0 1.5 multiply_subtract_fusion.16
  469.5 44.0 %collective-permute-done.8 = f32[2,128,2,512]{3,1,2,0:T(8,128)S(1)} collective-permute-done((f32[2,128,2,512]{3,1,2,0:T(8,128)}, f32[2,128,2,512]{3,1,2,0:T(8,128)S(1)}, u32[]{:S(2)}, u32[]{:S(2)}) %collective-permute-start.8) | collective-permute-done | bytes 1048608 | tf_op jit(solution)/shard_map/ppermute | solution.py:10
  514.5 2.1 fusion.3
  516.6 2.2 collective-permute-start.9
  519.1 48.2 %collective-permute-done.9 = f32[2,128,2,512]{3,1,2,0:T(8,128)S(1)} collective-permute-done((f32[2,128,2,512]{3,1,2,0:T(8,128)S(1)}, f32[2,128,2,512]{3,1,2,0:T(8,128)S(1)}, u32[]{:S(2)}, u32[]{:S(2)}) %collective-permute-start.9) | collective-permute-done | bytes 1048608 | tf_op jit(solution)/shard_map/ppermute | solution.py:10
  567.9 3.3 collective-permute-start.10
  571.5 22.8 %collective-permute-done.10 = f32[2,128,2,512]{3,1,2,0:T(8,128)S(1)} collective-permute-done((f32[2,128,2,512]{3,1,2,0:T(8,128)S(1)}, f32[2,128,2,512]{3,1,2,0:T(8,128)S(1)}, u32[]{:S(2)}, u32[]{:S(2)}) %collective-permute-start.10) | collective-permute-done | bytes 1048608 | tf_op jit(solution)/shard_map/ppermute | solution.py:10
  594.9 1.6 collective-permute-start.11
  596.8 21.9 %collective-permute-done.11 = f32[2,128,2,512]{3,1,2,0:T(8,128)S(1)} collective-permute-done((f32[2,128,2,512]{3,1,2,0:T(8,128)S(1)}, f32[2,128,2,512]{3,1,2,0:T(8,128)S(1)}, u32[]{:S(2)}, u32[]{:S(2)}) %collective-permute-start.11) | collective-permute-done | bytes 1048608 | tf_op jit(solution)/shard_map/ppermute | solution.py:10
  619.3 3.1 collective-permute-start.12
  622.7 21.0 %collective-permute-done.12 = f32[2,128,2,512]{3,1,2,0:T(8,128)S(1)} collective-permute-done((f32[2,128,2,512]{3,1,2,0:T(8,128)S(1)}, f32[2,128,2,512]{3,1,2,0:T(8,128)S(1)}, u32[]{:S(2)}, u32[]{:S(2)}) %collective-permute-start.12) | collective-permute-done | bytes 1048608 | tf_op jit(solution)/shard_map/ppermute | solution.py:10
  644.4 1.6 copy-done.13
  646.0 3.3 fusion.24
  649.3 44.2 %reduce-scatter.2.cloned.1.call-done = f32[128,1024]{1,0:T(8,128)} async-done(((f32[128,4096]{1,0:T(8,128)}), f32[128,1024]{1,0:T(8,128)}) %reduce-scatter.2.cloned.1.call-update) | async-done | bytes 524304 | tf_op jit(solution)/shard_map/reduce_scatter | solution.py:130
  693.5 1.8 convert_element_type.82
  (81 shorter events, 13.8 us)
Async XLA Ops:
  6.5 687.0 %reduce-scatter.2.cloned.1.call-start = ((), (), s32[]{:S(2)}) async-start(), calls=%async_computation.1 | async-start | bytes 2621440 | tf_op jit(solution)/shard_map/reduce_scatter | solution.py:130
  7.3 6.4 collective-permute-start
  14.9 1.2 copy-start.15
  15.1 0.9 copy-start.14
  18.0 51.3 %collective-permute-start.1 = (f32[2,128,4,512]{3,1,2,0:T(8,128)}, f32[2,128,4,512]{3,1,2,0:T(8,128)}, u32[]{:S(2)}, u32[]{:S(2)}) collective-permute-start(f32[2,128,4,512]{3,1,2,0:T(8,128)} %pad_maximum_fusion), channel_id=1, source_target_pairs={{0,128},{4,132},{8,136},{12,140},{16,144},{20,148},{24,152},{28,15... | collective-permute-start | bytes 6291464 | tf_op jit(solution)/shard_map/ppermute | solution.py:10
  71.7 4.1 copy-start
  75.8 45.3 %collective-permute-start.2 = (f32[2,128,4,512]{3,1,2,0:T(8,128)}, f32[2,128,4,512]{3,1,2,0:T(8,128)}, u32[]{:S(2)}, u32[]{:S(2)}) collective-permute-start(f32[2,128,4,512]{3,1,2,0:T(8,128)} %maximum_select_fusion), channel_id=1, source_target_pairs={{0,64},{4,68},{8,72},{12,76},{16,80},{20,84},{24,88},{28,92},{32,9... | collective-permute-start | bytes 6291464 | tf_op jit(solution)/shard_map/ppermute | solution.py:10
  124.6 1.2 copy-start.1
  130.7 44.2 %collective-permute-start.3 = (f32[2,128,4,512]{3,1,2,0:T(8,128)}, f32[2,128,4,512]{3,1,2,0:T(8,128)S(1)}, u32[]{:S(2)}, u32[]{:S(2)}) collective-permute-start(f32[2,128,4,512]{3,1,2,0:T(8,128)} %maximum_select_fusion.1), channel_id=1, source_target_pairs={{0,32},{4,36},{8,40},{12,44},{16,48},{20,52},{24,56},{28,60},{32,0... | collective-permute-start | bytes 6291464 | tf_op jit(solution)/shard_map/ppermute | solution.py:10
  174.9 2.8 copy-start.2
  181.0 94.1 %collective-permute-start.4 = (f32[2,128,4,512]{3,1,2,0:T(8,128)S(1)}, f32[2,128,4,512]{3,1,2,0:T(8,128)}, u32[]{:S(2)}, u32[]{:S(2)}) collective-permute-start(f32[2,128,4,512]{3,1,2,0:T(8,128)S(1)} %maximum_select_fusion.2), channel_id=1, source_target_pairs={{0,16},{4,20},{8,24},{12,28},{16,0},{20,4},{24,8},{28,12},{32,48},... | collective-permute-start | bytes 6291464 | tf_op jit(solution)/shard_map/ppermute | solution.py:10
  281.2 92.1 %collective-permute-start.5 = (f32[2,128,4,512]{3,1,2,0:T(8,128)}, f32[2,128,4,512]{3,1,2,0:T(8,128)S(1)}, u32[]{:S(2)}, u32[]{:S(2)}) collective-permute-start(f32[2,128,4,512]{3,1,2,0:T(8,128)} %maximum_select_fusion.3), channel_id=1, source_target_pairs={{0,8},{4,12},{8,0},{12,4},{16,24},{20,28},{24,16},{28,20},{32,40},... | collective-permute-start | bytes 6291464 | tf_op jit(solution)/shard_map/ppermute | solution.py:10
  373.3 2.8 copy-start.3
  379.4 45.5 %collective-permute-start.6 = (f32[2,128,4,512]{3,1,2,0:T(8,128)S(1)}, f32[2,128,4,512]{3,1,2,0:T(8,128)}, u32[]{:S(2)}, u32[]{:S(2)}) collective-permute-start(f32[2,128,4,512]{3,1,2,0:T(8,128)S(1)} %maximum_select_fusion.4), channel_id=1, source_target_pairs={{0,4},{4,0},{8,12},{12,8},{16,20},{20,16},{24,28},{28,24},{32,36},... | collective-permute-start | bytes 6291464 | tf_op jit(solution)/shard_map/ppermute | solution.py:10
  438.8 22.0 %copy-start.6 = (f32[1,128,2,512]{3,1,2,0:T(8,128)}, f32[1,128,2,512]{3,1,2,0:T(8,128)S(1)}, u32[]{:S(2)}) copy-start(f32[1,128,2,512]{3,1,2,0:T(8,128)S(1)} %get-tuple-element.5) | copy-start | bytes 1572868
  438.9 21.8 %collective-permute-start.7 = (f32[2,128,2,512]{3,1,2,0:T(8,128)S(1)}, f32[2,128,2,512]{3,1,2,0:T(8,128)S(1)}, u32[]{:S(2)}, u32[]{:S(2)}) collective-permute-start(f32[2,128,2,512]{3,1,2,0:T(8,128)S(1)} %pad_maximum_fusion.1), channel_id=1, source_target_pairs={{0,4},{4,0},{8,12},{12,8},{16,20},{20,16},{24,28},{28,24},{32,36},... | collective-permute-start | bytes 3145736 | tf_op jit(solution)/shard_map/ppermute | solution.py:10
  439.4 23.0 %copy-start.4 = (f32[1,128,2,512]{3,1,2,0:T(8,128)}, f32[1,128,2,512]{3,1,2,0:T(8,128)S(1)}, u32[]{:S(2)}) copy-start(f32[1,128,2,512]{3,1,2,0:T(8,128)S(1)} %add_bitcast_fusion) | copy-start | bytes 1572868
  460.9 1.5 copy-start.8
  460.9 1.5 copy-start.10
  462.4 51.0 %collective-permute-start.8 = (f32[2,128,2,512]{3,1,2,0:T(8,128)}, f32[2,128,2,512]{3,1,2,0:T(8,128)S(1)}, u32[]{:S(2)}, u32[]{:S(2)}) collective-permute-start(f32[2,128,2,512]{3,1,2,0:T(8,128)} %fusion.2), channel_id=1, source_target_pairs={{0,8},{4,12},{8,0},{12,4},{16,24},{20,28},{24,16},{28,20},{32,40},... | collective-permute-start | bytes 3145736 | tf_op jit(solution)/shard_map/ppermute | solution.py:10
  467.9 46.5 %copy-start.5 = (f32[1,128,2,512]{3,1,2,0:T(8,128)S(1)}, f32[1,128,2,512]{3,1,2,0:T(8,128)}, u32[]{:S(2)}) copy-start(f32[1,128,2,512]{3,1,2,0:T(8,128)} %copy-done.4) | copy-start | bytes 1572868
  467.9 46.5 %copy-start.7 = (f32[1,128,2,512]{3,1,2,0:T(8,128)S(1)}, f32[1,128,2,512]{3,1,2,0:T(8,128)}, u32[]{:S(2)}) copy-start(f32[1,128,2,512]{3,1,2,0:T(8,128)} %copy-done.6) | copy-start | bytes 1572868
  467.9 46.5 %copy-start.9 = (f32[1,128,2,512]{3,1,2,0:T(8,128)S(1)}, f32[1,128,2,512]{3,1,2,0:T(8,128)}, u32[]{:S(2)}) copy-start(f32[1,128,2,512]{3,1,2,0:T(8,128)} %copy-done.8) | copy-start | bytes 1572868
  467.9 46.5 %copy-start.11 = (f32[1,128,2,512]{3,1,2,0:T(8,128)S(1)}, f32[1,128,2,512]{3,1,2,0:T(8,128)}, u32[]{:S(2)}) copy-start(f32[1,128,2,512]{3,1,2,0:T(8,128)} %copy-done.10) | copy-start | bytes 1572868
  513.4 1.0 copy-start.12
  516.6 50.6 %collective-permute-start.9 = (f32[2,128,2,512]{3,1,2,0:T(8,128)S(1)}, f32[2,128,2,512]{3,1,2,0:T(8,128)S(1)}, u32[]{:S(2)}, u32[]{:S(2)}) collective-permute-start(f32[2,128,2,512]{3,1,2,0:T(8,128)S(1)} %fusion.3), channel_id=1, source_target_pairs={{0,16},{4,20},{8,24},{12,28},{16,0},{20,4},{24,8},{28,12},{32,48},... | collective-permute-start | bytes 3145736 | tf_op jit(solution)/shard_map/ppermute | solution.py:10
  567.9 26.4 %collective-permute-start.10 = (f32[2,128,2,512]{3,1,2,0:T(8,128)S(1)}, f32[2,128,2,512]{3,1,2,0:T(8,128)S(1)}, u32[]{:S(2)}, u32[]{:S(2)}) collective-permute-start(f32[2,128,2,512]{3,1,2,0:T(8,128)S(1)} %fusion.4), channel_id=1, source_target_pairs={{0,32},{4,36},{8,40},{12,44},{16,48},{20,52},{24,56},{28,60},{32,0... | collective-permute-start | bytes 3145736 | tf_op jit(solution)/shard_map/ppermute | solution.py:10
  594.9 23.7 %collective-permute-start.11 = (f32[2,128,2,512]{3,1,2,0:T(8,128)S(1)}, f32[2,128,2,512]{3,1,2,0:T(8,128)S(1)}, u32[]{:S(2)}, u32[]{:S(2)}) collective-permute-start(f32[2,128,2,512]{3,1,2,0:T(8,128)S(1)} %fusion.5), channel_id=1, source_target_pairs={{0,64},{4,68},{8,72},{12,76},{16,80},{20,84},{24,88},{28,92},{32,9... | collective-permute-start | bytes 3145736 | tf_op jit(solution)/shard_map/ppermute | solution.py:10
  619.3 24.3 %collective-permute-start.12 = (f32[2,128,2,512]{3,1,2,0:T(8,128)S(1)}, f32[2,128,2,512]{3,1,2,0:T(8,128)S(1)}, u32[]{:S(2)}, u32[]{:S(2)}) collective-permute-start(f32[2,128,2,512]{3,1,2,0:T(8,128)S(1)} %fusion.6), channel_id=1, source_target_pairs={{0,128},{4,132},{8,136},{12,140},{16,144},{20,148},{24,152},{28,15... | collective-permute-start | bytes 3145736 | tf_op jit(solution)/shard_map/ppermute | solution.py:10
  643.8 2.2 copy-start.13
  644.3 1.7 copy-start.16
Sparse Core Ops, SparseCore 0:
  649.4 44.0 reduce-scatter.1
where the time goes:
time: 703 us; the launch traced here: 702 us
  waiting for transfers between devices  585 us (83%)
  other arithmetic  54.2 us (8%)
  starting transfers between devices  29.9 us (4%)
  between operations  15.6 us (2%)
  matrix products  12.2 us (2%)
    ppermute x12, waiting for transfers between devices, from_partner(): lax.ppermute(x, axis, [(i, i ^ 1 << apart) for i in range(lax.axis_size(a...  541 us
    reduce_scatter x1, waiting for transfers between devices, body(): lax.psum_scatter(partial_value, 'chan', scatter_dimension=1, tiled=True)  44.2 us
    ppermute x12, starting transfers between devices, from_partner(): lax.ppermute(x, axis, [(i, i ^ 1 << apart) for i in range(lax.axis_size(a...  25.5 us
    select_n x6, other arithmetic, pair_forward(): signal_data = jnp.where(upper_bit == 1, turned, signal_data + partner)  21 us
    sub x6, other arithmetic, pair_forward(): turned = rotate(partner - signal_data, -math.pi * offset / half_span)  15.4 us
  transfers between devices with their start and end apart: 14, of which 13 were waited for; matrix products, arithmetic and copies ran while one was open for 1% of the time, Pallas kernels for 0%

commit v1 on v0

v1 whole, which is shorter than its diff:
```python
import functools
import math

import jax
import jax.numpy as jnp
import ml_dtypes
import numpy as np
from jax import lax
from jax.experimental import pallas as pl
from jax.experimental.pallas import tpu as pltpu
from jax.sharding import PartitionSpec as P

MESH = pl.DeviceIdType.MESH
F32 = jnp.float32
BF16 = jnp.bfloat16
HALO = 16
PARTS = 4


def transform_tables(blocks, tokens, group):
    length = blocks * tokens
    frequency = np.arange(blocks) + 0.25
    outer_angle = 2 * math.pi * np.outer(frequency, np.arange(blocks)) / blocks
    outer = np.stack([np.cos(outer_angle), np.sin(outer_angle)], axis=1).reshape(2 * blocks, blocks)
    first = np.kron(outer, np.eye(group))
    turn = 2 * math.pi * np.outer(frequency, np.arange(tokens)) / length
    turn = np.repeat(turn, group, axis=0)
    inner_angle = 2 * math.pi * np.outer(np.arange(tokens), np.arange(tokens)) / tokens
    cosine, sine = np.cos(inner_angle), np.sin(inner_angle)
    inner = np.block([[cosine, sine], [-sine, cosine]])
    back = np.block([[cosine, -sine], [sine, cosine]]) / length
    narrow = lambda table: table.astype(ml_dtypes.bfloat16)
    return (
        narrow(first),
        narrow(first.T.copy()),
        narrow(inner),
        narrow(back),
        np.cos(turn).astype(np.float32),
        np.sin(turn).astype(np.float32),
    )


def dot(a, b):
    return jnp.dot(a, b, preferred_element_type=F32)


def kernel(
    n,
    q_hbm,
    k_hbm,
    v_hbm,
    taps_hbm,
    filter_hbm,
    skip_hbm,
    weight_hbm,
    first_hbm,
    last_hbm,
    inner_hbm,
    back_hbm,
    cos_hbm,
    sin_hbm,
    out_ref,
    streams,
    taps,
    filt,
    skip,
    weight,
    first,
    last,
    inner,
    back,
    cosine,
    sine,
    halo,
    padded,
    q_short,
    skipped,
    send_h,
    send_p,
    send_y,
    recv_h,
    recv_p,
    recv_y,
    response,
    send_core,
    recv_core,
    send_cross,
    recv_cross,
    load_sem,
    halo_send,
    halo_recv,
    all_send,
    all_recv,
    core_send,
    core_recv,
    cross_send,
    cross_recv,
):
    me, chan = lax.axis_index("seq"), lax.axis_index("chan")
    core, high = lax.rem(chan, 2), lax.div(chan, 2)
    other_core = high * 2 + 1 - core
    other_high = (1 - high) * 2 + core
    tokens, channels = filt.shape
    group = channels // n
    columns = weight.shape[2]

    def block_of(y_high, y_core):
        return weight_hbm.at[:, pl.ds(pl.multiple_of((y_high * 2 + y_core) * columns, columns), columns)]

    pairs = [
        (filter_hbm, filt),
        (k_hbm, streams.at[1]),
        (v_hbm, streams.at[2]),
        (q_hbm, streams.at[0]),
        (taps_hbm, taps),
        (skip_hbm, skip),
        (first_hbm, first),
        (cos_hbm, cosine),
        (sin_hbm, sine),
        (inner_hbm, inner),
        (back_hbm, back),
        (last_hbm, last),
        (block_of(1 - high, 1 - core), weight.at[0]),
        (block_of(1 - high, core), weight.at[1]),
        (block_of(high, 1 - core), weight.at[2]),
        (block_of(high, core), weight.at[3]),
    ]
    loads = [pltpu.make_async_copy(src, dst, load_sem.at[i]) for i, (src, dst) in enumerate(pairs)]
    for load in loads[:4]:
        load.start()

    barrier = pltpu.get_barrier_semaphore()

    @pl.loop(1, n)
    def _(d):
        pl.semaphore_signal(barrier, inc=1, device_id=(lax.rem(me + d, n), chan), device_id_type=MESH)

    pl.semaphore_signal(barrier, inc=1, device_id=(me, other_core), device_id_type=MESH)
    pl.semaphore_signal(barrier, inc=1, device_id=(me, other_high), device_id_type=MESH)
    for load in loads[4:]:
        load.start()

    def exchange(source, target, index):
        @pl.loop(1, n)
        def _(d):
            peer = lax.rem(me + d, n)
            pltpu.make_async_remote_copy(
                src_ref=source.at[peer],
                dst_ref=target.at[me],
                send_sem=all_send.at[index],
                recv_sem=all_recv.at[index],
                device_id=(peer, chan),
                device_id_type=MESH,
            ).start()

        target[me] = source[me]

    def arrived(buffer, index):
        part = buffer.at[pl.ds(0, n - 1)]
        pltpu.make_async_copy(part, part, all_recv.at[index]).wait()

    def left(buffer, index):
        part = buffer.at[pl.ds(0, n - 1)]
        pltpu.make_async_copy(part, part, all_send.at[index]).wait()

    def to_channels(value, buffer):
        per = tokens // group
        for i in range(channels // tokens):
            turned = value[:, i * tokens : (i + 1) * tokens].T
            buffer[i * per : (i + 1) * per] = turned.reshape(per, group, tokens).astype(BF16)

    loads[0].wait()
    to_channels(filt[...], send_h)
    for load in loads[1:4]:
        load.wait()

    pl.semaphore_wait(barrier, n + 1)
    after = lax.rem(me + 1, n)
    rims = []
    for i in (1, 2, 0):
        rims.append(
            pltpu.make_async_remote_copy(
                src_ref=streams.at[i, pl.ds(tokens - HALO, HALO)],
                dst_ref=halo.at[i],
                send_sem=halo_send.at[i],
                recv_sem=halo_recv.at[i],
                device_id=(after, chan),
                device_id_type=MESH,
            )
        )
        rims[-1].start()
    exchange(send_h, recv_h, 0)

    for load in loads[4:6]:
        load.wait()
    inside = jnp.where(me > 0, 1.0, 0.0).astype(F32)

    def short(i):
        padded[0:HALO] = halo[i].astype(F32) * inside
        padded[HALO : HALO + tokens] = streams[i].astype(F32)
        total = taps[i, 0:1] * padded[HALO : HALO + tokens]
        for lag in range(1, taps.shape[1]):
            total += taps[i, lag : lag + 1] * padded[HALO - lag : HALO - lag + tokens]
        return total

    rims[0].wait_recv()
    rims[1].wait_recv()
    k_short = short(1)
    product = k_short * short(2)
    to_channels(product, send_p)
    exchange(send_p, recv_p, 1)
    skipped[...] = skip[...] * product
    rims[2].wait_recv()
    q_short[...] = short(0)

    for load in loads[6:]:
        load.wait()

    def split(value):
        value = value.reshape(n, 2, group, tokens)
        return value[:, 0].reshape(channels, tokens), value[:, 1].reshape(channels, tokens)

    def forward(buffer):
        signal = buffer[...].astype(F32).reshape(channels, tokens).astype(BF16)
        real, imag = split(dot(first[...], signal))
        turned = [real * cosine[...] - imag * sine[...], real * sine[...] + imag * cosine[...]]
        return dot(jnp.concatenate(turned, axis=1).astype(BF16), inner[...])

    arrived(recv_h, 0)
    response[...] = forward(recv_h)
    arrived(recv_p, 1)
    spectrum = forward(recv_p)
    p_real, p_imag = spectrum[:, :tokens], spectrum[:, tokens:]
    h_real, h_imag = response[:, :tokens], response[:, tokens:]
    filtered = [p_real * h_real - p_imag * h_imag, p_real * h_imag + p_imag * h_real]
    mixed = dot(jnp.concatenate(filtered, axis=1).astype(BF16), back[...])
    real, imag = mixed[:, :tokens], mixed[:, tokens:]
    turned = [real * cosine[...] + imag * sine[...], imag * cosine[...] - real * sine[...]]
    turned = [part.reshape(n, 1, group, tokens) for part in turned]
    turned = jnp.concatenate(turned, axis=1).reshape(2 * channels, tokens).astype(BF16)
    convolved = dot(last[...], turned)
    send_y[...] = convolved.reshape(n, group, tokens).astype(BF16)
    exchange(send_y, recv_y, 2)
    arrived(recv_y, 2)

    long_part = recv_y[...].astype(F32).reshape(channels, tokens)
    long_part = jnp.concatenate([long_part[i * tokens : (i + 1) * tokens].T for i in range(channels // tokens)], axis=1)
    gated = (q_short[...] * (long_part + skipped[...])).astype(BF16)

    width = columns // PARTS

    def project(i, part):
        return dot(gated, weight[i, :, part * width : (part + 1) * width])

    def core_copy(half, part):
        return pltpu.make_async_remote_copy(
            src_ref=send_core.at[half, part],
            dst_ref=recv_core.at[half, part],
            send_sem=core_send.at[half, part],
            recv_sem=core_recv.at[half, part],
            device_id=(me, other_core),
            device_id_type=MESH,
        )

    def cross_copy(part):
        return pltpu.make_async_remote_copy(
            src_ref=send_cross.at[part],
            dst_ref=recv_cross.at[part],
            send_sem=cross_send.at[part],
            recv_sem=cross_recv.at[part],
            device_id=(me, other_high),
            device_id_type=MESH,
        )

    for part in range(PARTS):
        send_core[0, part] = project(0, part).astype(BF16)
        core_copy(0, part).start()
    for part in range(PARTS):
        mine = project(1, part)
        core_copy(0, part).wait_recv()
        send_cross[part] = (mine + recv_core[0, part].astype(F32)).astype(BF16)
        cross_copy(part).start()
    for part in range(PARTS):
        send_core[1, part] = project(2, part).astype(BF16)
        core_copy(1, part).start()
    for part in range(PARTS):
        mine = project(3, part)
        core_copy(1, part).wait_recv()
        mine = mine + recv_core[1, part].astype(F32)
        cross_copy(part).wait_recv()
        out_ref[:, part * width : (part + 1) * width] = (mine + recv_cross[part].astype(F32)).astype(BF16)

    for rim in rims:
        rim.wait_send()
    left(send_h, 0)
    left(send_p, 1)
    left(send_y, 2)
    for part in range(PARTS):
        core_copy(0, part).wait_send()
        core_copy(1, part).wait_send()
        cross_copy(part).wait_send()


def body(n, q_stream, k_stream, v_stream, short_taps, long_filter, skip_gain, out_weight):
    tokens, channels = long_filter.shape
    rows, features = out_weight.shape
    columns = features // lax.axis_size("chan")
    group = channels // n
    tables = transform_tables(n, tokens, group)
    hbm = pl.BlockSpec(memory_space=pl.ANY)
    width = columns // PARTS
    slabs = pltpu.VMEM((n, group, tokens), BF16)
    scratch = [
        pltpu.VMEM((3, tokens, channels), BF16),
        pltpu.VMEM(short_taps.shape, F32),
        pltpu.VMEM((tokens, channels), F32),
        pltpu.VMEM((1, channels), F32),
        pltpu.VMEM((4, rows, columns), BF16),
        *[pltpu.VMEM(table.shape, table.dtype) for table in tables],
        pltpu.VMEM((3, HALO, channels), BF16),
        pltpu.VMEM((HALO + tokens, channels), F32),
        pltpu.VMEM((tokens, channels), F32),
        pltpu.VMEM((tokens, channels), F32),
        *[slabs] * 6,
        pltpu.VMEM((channels, 2 * tokens), F32),
        pltpu.VMEM((2, PARTS, tokens, width), BF16),
        pltpu.VMEM((2, PARTS, tokens, width), BF16),
        pltpu.VMEM((PARTS, tokens, width), BF16),
        pltpu.VMEM((PARTS, tokens, width), BF16),
        pltpu.SemaphoreType.DMA((16,)),
        pltpu.SemaphoreType.DMA((3,)),
        pltpu.SemaphoreType.DMA((3,)),
        pltpu.SemaphoreType.DMA((3,)),
        pltpu.SemaphoreType.DMA((3,)),
        pltpu.SemaphoreType.DMA((2, PARTS)),
        pltpu.SemaphoreType.DMA((2, PARTS)),
        pltpu.SemaphoreType.DMA((PARTS,)),
        pltpu.SemaphoreType.DMA((PARTS,)),
    ]
    return pl.pallas_call(
        functools.partial(kernel, n),
        out_shape=jax.ShapeDtypeStruct((tokens, columns), BF16),
        in_specs=[hbm] * 13,
        out_specs=pl.BlockSpec(memory_space=pltpu.VMEM),
        scratch_shapes=scratch,
        compiler_params=pltpu.CompilerParams(
            collective_id=0, has_side_effects=True, vmem_limit_bytes=48 * 1024 * 1024
        ),
    )(
        q_stream,
        k_stream,
        v_stream,
        short_taps,
        long_filter,
        skip_gain.reshape(1, channels),
        out_weight,
        *tables,
    )


def solution(mesh):
    in_specs = (
        P("seq", "chan"),
        P("seq", "chan"),
        P("seq", "chan"),
        P(None, None, "chan"),
        P("seq", "chan"),
        P("chan"),
        P("chan", None),
    )
    return jax.shard_map(
        functools.partial(body, mesh.shape["seq"]),
        mesh=mesh,
        in_specs=in_specs,
        out_specs=P("seq", "chan"),
        check_vma=False,
    )
```

time: 703 us -> 56.5 us (0.08)
  waiting for transfers between devices: 585 us -> 0 us
  other arithmetic: 54.2 us -> 0 us
  Pallas kernels: 0 us -> 44.1 us
  starting transfers between devices: 29.9 us -> 0 us
  between operations: 15.6 us -> 0.02 us
  matrix products: 12.2 us -> 0 us
    ppermute x13 -> x0, waiting for transfers between devices: 541 us -> none  [the longest x12 541 us: from_partner(): lax.ppermute(x, axis, [(i, i ^ 1 << apart) for i in range(lax.axis_size(a...]
    reduce_scatter x1 -> x0, waiting for transfers between devices: 44.2 us -> none  [body(): lax.psum_scatter(partial_value, 'chan', scatter_dimension=1, tiled=True)]
    pallas_call x0 -> x1, Pallas kernels: none -> 44.1 us  [body(): pl.pallas_call(functools.partial(kernel, n), out_shape=jax.ShapeDtypeStru...]
    ppermute x13 -> x0, starting transfers between devices: 29.9 us -> none  [the longest x12 25.5 us: from_partner(): lax.ppermute(x, axis, [(i, i ^ 1 << apart) for i in range(lax.axis_size(a...]
    select_n x12 -> x0, other arithmetic: 26.6 us -> none  [the longest x6 21 us: pair_forward(): signal_data = jnp.where(upper_bit == 1, turned, signal_data + partner)]
    sub x24 -> x0, other arithmetic: 20.2 us -> none  [the longest x6 15.4 us: pair_forward(): turned = rotate(partner - signal_data, -math.pi * offset / half_span)]
    dot_general x9 -> x0, matrix products: 12.2 us -> none  [the longest x1 3.3 us: body(): jnp.dot(gated_values, out_weight, preferred_element_type=jnp.float32)]
    unnamed x37 -> x25, local copies, waits for them, and re-layouts: 4.17 us -> 11.9 us
  transfers between devices with their start and end apart: 14 -> 0, of which waited for: 13 -> 0; matrix products, arithmetic and copies ran while one was open for 1% -> 0% of each run, Pallas kernels for 0% -> 0%
where the time goes in v1:
time: 56.5 us; the launch traced here: 56 us
  Pallas kernels  44.1 us (78%)
  local copies, waits for them, and re-layouts  11.9 us (21%)
    pallas_call x1, Pallas kernels, body(): pl.pallas_call(functools.partial(kernel, n), out_shape=jax.ShapeDtypeStru...  44.1 us
    unnamed x25, local copies, waits for them, and re-layouts  11.9 us

profile of v1, /device:TPU:1, one launch (start us, length us, event | category | flops | bytes accessed | tf_op | source)
XLA Modules:
  0.0 56.0 jit_solution(7691950781007947084)
XLA Ops:
  0.0 0.0 copy-start
  0.0 1.2 %copy-done = bf16[512,1024]{1,0:T(8,128)(2,1)S(1)} copy-done((bf16[512,1024]{1,0:T(8,128)(2,1)S(1)}, bf16[512,1024]{1,0:T(8,128)(2,1)}, u32[]{:S(2)}) %copy-start) | copy-done | bytes 1048600
  1.2 0.0 copy-start.1
  1.2 1.2 %copy-done.1 = bf16[1024,512]{1,0:T(8,128)(2,1)S(1)} copy-done((bf16[1024,512]{1,0:T(8,128)(2,1)S(1)}, bf16[1024,512]{1,0:T(8,128)(2,1)}, u32[]{:S(2)}) %copy-start.1) | copy-done | bytes 1048600
  2.5 0.0 copy-start.2
  2.5 0.9 %copy-done.2 = f32[128,512]{1,0:T(8,128)S(1)} copy-done((f32[128,512]{1,0:T(8,128)S(1)}, f32[128,512]{1,0:T(8,128)}, u32[]{:S(2)}) %copy-start.2) | copy-done | bytes 262168
  3.4 0.0 copy-start.3
  3.4 0.9 %copy-done.3 = f32[512,128]{1,0:T(8,128)S(1)} copy-done((f32[512,128]{1,0:T(8,128)S(1)}, f32[512,128]{1,0:T(8,128)}, u32[]{:S(2)}) %copy-start.3) | copy-done | bytes 262168
  4.4 0.0 copy-start.4
  4.4 0.9 %copy-done.4 = f32[512,128]{1,0:T(8,128)S(1)} copy-done((f32[512,128]{1,0:T(8,128)S(1)}, f32[512,128]{1,0:T(8,128)}, u32[]{:S(2)}) %copy-start.4) | copy-done | bytes 262168
  5.3 0.0 copy-start.5
  5.3 0.9 %copy-done.5 = bf16[128,512]{1,0:T(8,128)(2,1)S(1)} copy-done((bf16[128,512]{1,0:T(8,128)(2,1)S(1)}, bf16[128,512]{1,0:T(8,128)(2,1)}, u32[]{:S(2)}) %copy-start.5) | copy-done | bytes 131096
  6.2 0.0 copy-start.6
  6.2 0.9 %copy-done.6 = bf16[128,512]{1,0:T(8,128)(2,1)S(1)} copy-done((bf16[128,512]{1,0:T(8,128)(2,1)S(1)}, bf16[128,512]{1,0:T(8,128)(2,1)}, u32[]{:S(2)}) %copy-start.6) | copy-done | bytes 131096
  7.1 0.0 copy-start.7
  7.1 0.9 %copy-done.7 = bf16[128,512]{1,0:T(8,128)(2,1)S(1)} copy-done((bf16[128,512]{1,0:T(8,128)(2,1)S(1)}, bf16[128,512]{1,0:T(8,128)(2,1)}, u32[]{:S(2)}) %copy-start.7) | copy-done | bytes 131096
  8.0 0.0 copy-start.8
  8.0 0.9 %copy-done.8 = bf16[256,256]{1,0:T(8,128)(2,1)S(1)} copy-done((bf16[256,256]{1,0:T(8,128)(2,1)S(1)}, bf16[256,256]{1,0:T(8,128)(2,1)}, u32[]{:S(2)}) %copy-start.8) | copy-done | bytes 131096
  8.9 0.0 copy-start.9
  8.9 0.9 %copy-done.9 = bf16[256,256]{1,0:T(8,128)(2,1)S(1)} copy-done((bf16[256,256]{1,0:T(8,128)(2,1)S(1)}, bf16[256,256]{1,0:T(8,128)(2,1)}, u32[]{:S(2)}) %copy-start.9) | copy-done | bytes 131096
  9.8 0.0 copy-start.10
  9.8 0.7 %copy-done.10 = f32[3,3,512]{2,1,0:T(4,128)S(1)} copy-done((f32[3,3,512]{2,1,0:T(4,128)S(1)}, f32[3,3,512]{2,1,0:T(4,128)}, u32[]{:S(2)}) %copy-start.10) | copy-done | bytes 18456
  10.6 0.0 copy-start.11
  10.6 0.7 %copy-done.11 = f32[512]{0:T(512)S(1)} copy-done((f32[512]{0:T(512)S(1)}, f32[512]{0:T(512)}, u32[]{:S(2)}) %copy-start.11) | copy-done | bytes 2072
  11.2 44.1 %shard_map.127 = bf16[128,1024]{1,0:T(8,128)(2,1)S(1)} custom-call(bf16[128,512]{1,0:T(8,128)(2,1)S(1)} %copy-done.5, bf16[128,512]{1,0:T(8,128)(2,1)S(1)} %copy-done.6, bf16[128,512]{1,0:T(8,128)(2,1)S(1)} %copy-done.7, f32[3,3,512]{2,1,0:T(4,128)S(1)} %copy-done.10, f32[128,512]{1,0:T(8,128)S(1)} %copy-done.2, f32[1,512]{1,0:T(1,128)S(1)} %bitcast.1, ...), custom_call_target="tpu_custom_call" | custom-call | tf_op jit(solution)/shard_map/pallas_call | solution.py:340
  55.3 0.7 %copy.15 = bf16[128,1024]{1,0:T(8,128)(2,1)} copy(bf16[128,1024]{1,0:T(8,128)(2,1)S(1)} %shard_map.127) | data formatting | bytes 524288
Async XLA Ops:
  0.0 1.2 %copy-start = (bf16[512,1024]{1,0:T(8,128)(2,1)S(1)}, bf16[512,1024]{1,0:T(8,128)(2,1)}, u32[]{:S(2)}) copy-start(bf16[512,1024]{1,0:T(8,128)(2,1)} %constant.13.clone.last_hbm) | copy-start | bytes 3145732
  1.2 1.2 %copy-start.1 = (bf16[1024,512]{1,0:T(8,128)(2,1)S(1)}, bf16[1024,512]{1,0:T(8,128)(2,1)}, u32[]{:S(2)}) copy-start(bf16[1024,512]{1,0:T(8,128)(2,1)} %constant.12.clone.first_hbm) | copy-start | bytes 3145732
  2.5 0.9 %copy-start.2 = (f32[128,512]{1,0:T(8,128)S(1)}, f32[128,512]{1,0:T(8,128)}, u32[]{:S(2)}) copy-start(f32[128,512]{1,0:T(8,128)} %filter_hbm.1) | copy-start | bytes 786436
  3.4 0.9 %copy-start.3 = (f32[512,128]{1,0:T(8,128)S(1)}, f32[512,128]{1,0:T(8,128)}, u32[]{:S(2)}) copy-start(f32[512,128]{1,0:T(8,128)} %constant.17.clone.sin_hbm) | copy-start | bytes 786436
  4.4 0.9 %copy-start.4 = (f32[512,128]{1,0:T(8,128)S(1)}, f32[512,128]{1,0:T(8,128)}, u32[]{:S(2)}) copy-start(f32[512,128]{1,0:T(8,128)} %constant.16.clone.cos_hbm) | copy-start | bytes 786436
  5.3 0.9 %copy-start.5 = (bf16[128,512]{1,0:T(8,128)(2,1)S(1)}, bf16[128,512]{1,0:T(8,128)(2,1)}, u32[]{:S(2)}) copy-start(bf16[128,512]{1,0:T(8,128)(2,1)} %q_hbm.1) | copy-start | bytes 393220
  6.2 0.9 %copy-start.6 = (bf16[128,512]{1,0:T(8,128)(2,1)S(1)}, bf16[128,512]{1,0:T(8,128)(2,1)}, u32[]{:S(2)}) copy-start(bf16[128,512]{1,0:T(8,128)(2,1)} %k_hbm.1) | copy-start | bytes 393220
  7.1 0.9 %copy-start.7 = (bf16[128,512]{1,0:T(8,128)(2,1)S(1)}, bf16[128,512]{1,0:T(8,128)(2,1)}, u32[]{:S(2)}) copy-start(bf16[128,512]{1,0:T(8,128)(2,1)} %v_hbm.1) | copy-start | bytes 393220
  8.0 0.9 %copy-start.8 = (bf16[256,256]{1,0:T(8,128)(2,1)S(1)}, bf16[256,256]{1,0:T(8,128)(2,1)}, u32[]{:S(2)}) copy-start(bf16[256,256]{1,0:T(8,128)(2,1)} %constant.15.clone.back_hbm) | copy-start | bytes 393220
  8.9 0.9 %copy-start.9 = (bf16[256,256]{1,0:T(8,128)(2,1)S(1)}, bf16[256,256]{1,0:T(8,128)(2,1)}, u32[]{:S(2)}) copy-start(bf16[256,256]{1,0:T(8,128)(2,1)} %constant.14.clone.inner_hbm) | copy-start | bytes 393220
  9.8 0.7 %copy-start.10 = (f32[3,3,512]{2,1,0:T(4,128)S(1)}, f32[3,3,512]{2,1,0:T(4,128)}, u32[]{:S(2)}) copy-start(f32[3,3,512]{2,1,0:T(4,128)} %taps_hbm.1) | copy-start | bytes 55300
  10.6 0.7 %copy-start.11 = (f32[512]{0:T(512)S(1)}, f32[512]{0:T(512)}, u32[]{:S(2)}) copy-start(f32[512]{0:T(512)} %param.18) | copy-start | bytes 6148

commit v2 on v1

v2 whole, which is shorter than its diff:
```python
import functools
import math

import jax
import jax.numpy as jnp
import ml_dtypes
import numpy as np
from jax import lax
from jax.experimental import pallas as pl
from jax.experimental.pallas import tpu as pltpu
from jax.sharding import PartitionSpec as P

MESH = pl.DeviceIdType.MESH
F32 = jnp.float32
BF16 = jnp.bfloat16
EDGE = 8
PARTS = 4
DEPTH = 8


def transform_tables(blocks, tokens):
    length = blocks * tokens
    frequency = np.arange(blocks) + 0.25
    outer_angle = 2 * math.pi * np.outer(frequency, np.arange(blocks)) / blocks
    outer = np.concatenate([np.cos(outer_angle), np.sin(outer_angle)])
    turn = 2 * math.pi * np.outer(frequency, np.arange(tokens)) / length
    inner_angle = 2 * math.pi * np.outer(np.arange(tokens), np.arange(tokens)) / tokens
    cosine, sine = np.cos(inner_angle), np.sin(inner_angle)
    inner = np.block([[cosine, sine], [-sine, cosine]])
    back = np.block([[cosine, -sine], [sine, cosine]]) / length
    matrices = [table.astype(ml_dtypes.bfloat16) for table in (outer, outer.T.copy(), inner, back)]
    return (*matrices, np.cos(turn).astype(np.float32), np.sin(turn).astype(np.float32))


def dot(a, b):
    return jnp.dot(a, b, preferred_element_type=F32)


def kernel(
    n,
    q_hbm,
    k_hbm,
    v_hbm,
    taps_hbm,
    filter_hbm,
    skip_hbm,
    weight_hbm,
    first_hbm,
    last_hbm,
    inner_hbm,
    back_hbm,
    cos_hbm,
    sin_hbm,
    out_ref,
    streams,
    taps,
    filt,
    skip,
    weight,
    first,
    last,
    inner,
    back,
    cosine,
    sine,
    halo_out,
    halo_in,
    tail,
    padded,
    product,
    q_short,
    skipped,
    send_h,
    send_p,
    send_y,
    recv_h,
    recv_p,
    recv_y,
    response,
    flat,
    send_core,
    recv_core,
    send_cross,
    recv_cross,
    load_sem,
    halo_send,
    halo_recv,
    all_send,
    all_recv,
    core_send,
    core_recv,
    cross_send,
    cross_recv,
):
    me, chan = lax.axis_index("seq"), lax.axis_index("chan")
    core, high = lax.rem(chan, 2), lax.div(chan, 2)
    other_core = high * 2 + 1 - core
    other_high = (1 - high) * 2 + core
    tokens, channels = filt.shape
    group = channels // n
    columns = weight.shape[2]

    def block_of(y_high, y_core):
        return weight_hbm.at[:, pl.ds(pl.multiple_of((y_high * 2 + y_core) * columns, columns), columns)]

    pairs = [
        (k_hbm, streams.at[1]),
        (v_hbm, streams.at[2]),
        (taps_hbm, taps),
        (filter_hbm, filt),
        (q_hbm, streams.at[0]),
        (skip_hbm, skip),
        (first_hbm, first),
        (cos_hbm, cosine),
        (sin_hbm, sine),
        (inner_hbm, inner),
        (back_hbm, back),
        (last_hbm, last),
        (block_of(1 - high, 1 - core), weight.at[0]),
        (block_of(1 - high, core), weight.at[1]),
        (block_of(high, 1 - core), weight.at[2]),
        (block_of(high, core), weight.at[3]),
    ]
    loads = [pltpu.make_async_copy(src, dst, load_sem.at[i]) for i, (src, dst) in enumerate(pairs)]
    for load in loads[:6]:
        load.start()

    barrier = pltpu.get_barrier_semaphore()

    @pl.loop(1, n)
    def _(d):
        pl.semaphore_signal(barrier, inc=1, device_id=(lax.rem(me + d, n), chan), device_id_type=MESH)

    pl.semaphore_signal(barrier, inc=1, device_id=(me, other_core), device_id_type=MESH)
    pl.semaphore_signal(barrier, inc=1, device_id=(me, other_high), device_id_type=MESH)
    for load in loads[6:12]:
        load.start()

    def exchange(source, target, index):
        def send(peer):
            pltpu.make_async_remote_copy(
                src_ref=source.at[peer],
                dst_ref=target.at[me],
                send_sem=all_send.at[index],
                recv_sem=all_recv.at[index],
                device_id=(peer, chan),
                device_id_type=MESH,
            ).start()

        place, depth = lax.div(me, DEPTH), lax.rem(me, DEPTH)
        across, pair = lax.div(place, 2), lax.rem(place, 2)
        for step_across, step_pair in ((2, 1), (2, 0), (1, 1), (3, 1), (1, 0), (3, 0), (0, 1), (0, 0)):
            line = (lax.rem(across + step_across, n // DEPTH // 2) * 2 + lax.rem(pair + step_pair, 2)) * DEPTH

            @pl.loop(0, DEPTH if step_across + step_pair else DEPTH - 1)
            def _(i):
                far = DEPTH // 2 - lax.div(i + 1, 2)
                step = jnp.where(lax.rem(i, 2) == 1, far, DEPTH - far)
                send(line + lax.rem(depth + step, DEPTH))

        target[me] = source[me]

    def arrived(buffer, index):
        part = buffer.at[pl.ds(0, n - 1)]
        pltpu.make_async_copy(part, part, all_recv.at[index]).wait()

    def left(buffer, index):
        part = buffer.at[pl.ds(0, n - 1)]
        pltpu.make_async_copy(part, part, all_send.at[index]).wait()

    def to_channels(value, buffer):
        per = tokens // group
        for i in range(channels // tokens):
            turned = value[:, i * tokens : (i + 1) * tokens].T
            buffer[i * per : (i + 1) * per] = turned.reshape(per, group, tokens).astype(BF16)

    edge = EDGE

    def short(i, rows):
        total = taps[i, 0:1] * padded[i, edge : edge + rows]
        for lag in range(1, taps.shape[1]):
            total += taps[i, lag : lag + 1] * padded[i, edge - lag : edge - lag + rows]
        return total

    def fill(i):
        padded[i, 0:edge] = jnp.zeros((edge, channels), F32)
        padded[i, edge : edge + tokens] = streams[i].astype(F32)

    for load in loads[0:3]:
        load.wait()
    fill(1)
    fill(2)
    product[...] = short(1, tokens) * short(2, tokens)
    to_channels(product[...], send_p)
    loads[3].wait()
    to_channels(filt[...], send_h)
    loads[4].wait()
    fill(0)

    rim = taps.shape[1] - 1
    tail[...] = jnp.zeros(tail.shape, F32)
    for i in range(3):
        tail[i * rim : (i + 1) * rim] = padded[i, edge + tokens - rim : edge + tokens]
    halo_out[...] = tail[...].astype(BF16)

    pl.semaphore_wait(barrier, n + 1)
    rims = pltpu.make_async_remote_copy(
        src_ref=halo_out,
        dst_ref=halo_in,
        send_sem=halo_send,
        recv_sem=halo_recv,
        device_id=(lax.rem(me + 1, n), chan),
        device_id_type=MESH,
    )
    rims.start()
    exchange(send_h, recv_h, 0)

    inside = jnp.where(me > 0, 1.0, 0.0).astype(F32)

    rims.wait_recv()
    tail[...] = halo_in[...].astype(F32) * inside
    for i in range(3):
        padded[i, edge - rim : edge] = tail[i * rim : (i + 1) * rim]
    head = short(1, edge) * short(2, edge)
    product[0:edge] = head
    for i in range(channels // tokens):
        per = tokens // group
        turned = head[:, i * tokens : (i + 1) * tokens].T.reshape(per, group, edge).astype(BF16)
        send_p[i * per : (i + 1) * per, :, 0:edge] = turned
    exchange(send_p, recv_p, 1)
    for load in loads[12:]:
        load.start()
    loads[5].wait()
    skipped[...] = skip[...] * product[...]
    q_short[...] = short(0, tokens)

    for load in loads[6:12]:
        load.wait()

    def forward(buffer):
        flat[...] = buffer[...].astype(F32).reshape(channels, tokens)
        signal = [flat[pl.ds(c, n, stride=group)].astype(BF16) for c in range(group)]
        stage = dot(first[...], jnp.concatenate(signal, axis=1))
        turned = []
        for c in range(group):
            real, imag = stage[:n, c * tokens : (c + 1) * tokens], stage[n:, c * tokens : (c + 1) * tokens]
            pair = [real * cosine[...] - imag * sine[...], real * sine[...] + imag * cosine[...]]
            turned.append(jnp.concatenate(pair, axis=1).astype(BF16))
        return dot(jnp.concatenate(turned, axis=0), inner[...])

    arrived(recv_h, 0)
    response[...] = forward(recv_h)
    arrived(recv_p, 1)
    spectrum = forward(recv_p)
    p_real, p_imag = spectrum[:, :tokens], spectrum[:, tokens:]
    h_real, h_imag = response[:, :tokens], response[:, tokens:]
    filtered = [p_real * h_real - p_imag * h_imag, p_real * h_imag + p_imag * h_real]
    mixed = dot(jnp.concatenate(filtered, axis=1).astype(BF16), back[...])
    turned = []
    for c in range(group):
        real, imag = mixed[c * n : (c + 1) * n, :tokens], mixed[c * n : (c + 1) * n, tokens:]
        pair = [real * cosine[...] + imag * sine[...], imag * cosine[...] - real * sine[...]]
        turned.append(jnp.concatenate(pair, axis=0).astype(BF16))
    convolved = dot(last[...], jnp.concatenate(turned, axis=1))
    for c in range(group):
        flat[pl.ds(c, n, stride=group)] = convolved[:, c * tokens : (c + 1) * tokens]
    send_y[...] = flat[...].reshape(n, group, tokens).astype(BF16)
    exchange(send_y, recv_y, 2)
    arrived(recv_y, 2)

    long_part = recv_y[...].astype(F32).reshape(channels, tokens)
    long_part = jnp.concatenate([long_part[i * tokens : (i + 1) * tokens].T for i in range(channels // tokens)], axis=1)
    gated = (q_short[...] * (long_part + skipped[...])).astype(BF16)

    width = columns // PARTS

    def project(i, part):
        return dot(gated, weight[i, :, part * width : (part + 1) * width])

    def core_copy(half, part):
        return pltpu.make_async_remote_copy(
            src_ref=send_core.at[half, part],
            dst_ref=recv_core.at[half, part],
            send_sem=core_send.at[half, part],
            recv_sem=core_recv.at[half, part],
            device_id=(me, other_core),
            device_id_type=MESH,
        )

    def cross_copy(part):
        return pltpu.make_async_remote_copy(
            src_ref=send_cross.at[part],
            dst_ref=recv_cross.at[part],
            send_sem=cross_send.at[part],
            recv_sem=cross_recv.at[part],
            device_id=(me, other_high),
            device_id_type=MESH,
        )

    for load in loads[12:]:
        load.wait()
    kept = []
    for part in range(PARTS):
        send_core[0, part] = project(0, part).astype(BF16)
        core_copy(0, part).start()
        kept.append(project(1, part))
    for part in range(PARTS):
        core_copy(0, part).wait_recv()
        send_cross[part] = (kept[part] + recv_core[0, part].astype(F32)).astype(BF16)
        cross_copy(part).start()
    for part in range(PARTS):
        send_core[1, part] = project(2, part).astype(BF16)
        core_copy(1, part).start()
    for part in range(PARTS):
        mine = project(3, part)
        core_copy(1, part).wait_recv()
        mine = mine + recv_core[1, part].astype(F32)
        cross_copy(part).wait_recv()
        out_ref[:, part * width : (part + 1) * width] = (mine + recv_cross[part].astype(F32)).astype(BF16)

    rims.wait_send()
    left(send_h, 0)
    left(send_p, 1)
    left(send_y, 2)
    for part in range(PARTS):
        core_copy(0, part).wait_send()
        core_copy(1, part).wait_send()
        cross_copy(part).wait_send()


def body(n, q_stream, k_stream, v_stream, short_taps, long_filter, skip_gain, out_weight):
    tokens, channels = long_filter.shape
    rows, features = out_weight.shape
    columns = features // lax.axis_size("chan")
    group = channels // n
    tables = transform_tables(n, tokens)
    hbm = pl.BlockSpec(memory_space=pltpu.HBM)
    operands = [
        q_stream,
        k_stream,
        v_stream,
        short_taps,
        long_filter,
        skip_gain.reshape(1, channels),
        out_weight,
        *tables,
    ]
    width = columns // PARTS
    slabs = pltpu.VMEM((n, group, tokens), BF16)
    scratch = [
        pltpu.VMEM((3, tokens, channels), BF16),
        pltpu.VMEM(short_taps.shape, F32),
        pltpu.VMEM((tokens, channels), F32),
        pltpu.VMEM((1, channels), F32),
        pltpu.VMEM((4, rows, columns), BF16),
        *[pltpu.VMEM(table.shape, table.dtype) for table in tables],
        pltpu.VMEM((EDGE, channels), BF16),
        pltpu.VMEM((EDGE, channels), BF16),
        pltpu.VMEM((EDGE, channels), F32),
        pltpu.VMEM((3, EDGE + tokens, channels), F32),
        pltpu.VMEM((tokens, channels), F32),
        pltpu.VMEM((tokens, channels), F32),
        pltpu.VMEM((tokens, channels), F32),
        *[slabs] * 6,
        pltpu.VMEM((channels, 2 * tokens), F32),
        pltpu.VMEM((channels, tokens), F32),
        pltpu.VMEM((2, PARTS, tokens, width), BF16),
        pltpu.VMEM((2, PARTS, tokens, width), BF16),
        pltpu.VMEM((PARTS, tokens, width), BF16),
        pltpu.VMEM((PARTS, tokens, width), BF16),
        pltpu.SemaphoreType.DMA((16,)),
        pltpu.SemaphoreType.DMA,
        pltpu.SemaphoreType.DMA,
        pltpu.SemaphoreType.DMA((3,)),
        pltpu.SemaphoreType.DMA((3,)),
        pltpu.SemaphoreType.DMA((2, PARTS)),
        pltpu.SemaphoreType.DMA((2, PARTS)),
        pltpu.SemaphoreType.DMA((PARTS,)),
        pltpu.SemaphoreType.DMA((PARTS,)),
    ]
    return pl.pallas_call(
        functools.partial(kernel, n),
        out_shape=pltpu.VMEM((tokens, columns), BF16),
        in_specs=[hbm] * 13,
        out_specs=pl.BlockSpec(memory_space=pltpu.VMEM),
        scratch_shapes=scratch,
        compiler_params=pltpu.CompilerParams(
            collective_id=0, has_side_effects=True, vmem_limit_bytes=40 * 1024 * 1024
        ),
    )(*[pltpu.with_memory_space_constraint(jnp.asarray(each), pltpu.HBM) for each in operands])


def solution(mesh):
    in_specs = (
        P("seq", "chan"),
        P("seq", "chan"),
        P("seq", "chan"),
        P(None, None, "chan"),
        P("seq", "chan"),
        P("chan"),
        P("chan", None),
    )
    return jax.shard_map(
        functools.partial(body, mesh.shape["seq"]),
        mesh=mesh,
        in_specs=in_specs,
        out_specs=P("seq", "chan"),
        check_vma=False,
    )
```

time: 56.5 us -> 41.8 us (0.74)
  local copies, waits for them, and re-layouts: 11.9 us -> 0.71 us
  Pallas kernels: 44.1 us -> 41 us
    unnamed x25 -> x1, local copies, waits for them, and re-layouts: 11.9 us -> 0.71 us
    pallas_call x1, Pallas kernels: 44.1 us -> 41 us  [body(): pl.pallas_call(functools.partial(kernel, n), out_shape=pltpu.VMEM((tokens...]
where the time goes in v2:
time: 41.8 us
  Pallas kernels  41 us (98%)
  local copies, waits for them, and re-layouts  0.71 us (2%)
    pallas_call x1, Pallas kernels, body(): pl.pallas_call(functools.partial(kernel, n), out_shape=pltpu.VMEM((tokens...  41 us

profile of v2, /device:TPU:1, one launch (start us, length us, event | category | flops | bytes accessed | tf_op | source)
XLA Modules:
  0.0 41.8 jit_solution(1534862714869996483)
XLA Ops:
  0.0 41.0 %shard_map.127 = bf16[128,1024]{1,0:T(8,128)(2,1)S(1)} custom-call(bf16[128,512]{1,0:T(8,128)(2,1)} %q_hbm.1, bf16[128,512]{1,0:T(8,128)(2,1)} %k_hbm.1, bf16[128,512]{1,0:T(8,128)(2,1)} %v_hbm.1, f32[3,3,512]{2,1,0:T(4,128)} %taps_hbm.1, f32[128,512]{1,0:T(8,128)} %filter_hbm.1, f32[1,512]{1,0:T(1,128)} %bitcast.1, bf16[512,4096]{1,0:T(8,128)(2,1)} %weight_hbm.1, ...), custom_call_target="tpu_custom_call" | custom-call | tf_op jit(solution)/shard_map/pallas_call | solution.py:381
  41.0 0.7 %copy.15 = bf16[128,1024]{1,0:T(8,128)(2,1)} copy(bf16[128,1024]{1,0:T(8,128)(2,1)S(1)} %shard_map.127) | data formatting | bytes 524288

commit v3 on v2

--- a/solution.py
+++ b/solution.py
@@ -14,7 +14,7 @@
 F32 = jnp.float32
 BF16 = jnp.bfloat16
 EDGE = 8
-PARTS = 4
+PARTS = 2
 DEPTH = 8
 
 
@@ -56,7 +56,8 @@
     taps,
     filt,
     skip,
-    weight,
+    cross_weight,
+    own_weight,
     first,
     last,
     inner,
@@ -78,8 +79,9 @@
     recv_y,
     response,
     flat,
-    send_core,
-    recv_core,
+    gated,
+    mine,
+    own,
     send_cross,
     recv_cross,
     load_sem,
@@ -87,21 +89,35 @@
     halo_recv,
     all_send,
     all_recv,
-    core_send,
-    core_recv,
+    weight_send,
+    weight_recv,
+    gated_send,
+    gated_recv,
     cross_send,
     cross_recv,
 ):
     me, chan = lax.axis_index("seq"), lax.axis_index("chan")
     core, high = lax.rem(chan, 2), lax.div(chan, 2)
     other_core = high * 2 + 1 - core
-    other_high = (1 - high) * 2 + core
+    across = ((1 - high) * 2 + 1, (1 - high) * 2)
     tokens, channels = filt.shape
     group = channels // n
-    columns = weight.shape[2]
-
-    def block_of(y_high, y_core):
-        return weight_hbm.at[:, pl.ds(pl.multiple_of((y_high * 2 + y_core) * columns, columns), columns)]
+    columns = own_weight.shape[2]
+
+    half = columns // 2
+
+    def weight_part(feature_block, start, width):
+        return weight_hbm.at[:, pl.ds(pl.multiple_of(feature_block * columns + start, half), width)]
+
+    def parts_for(which):
+        return [
+            weight_part((1 - high) * 2 + 1, which * half, half),
+            weight_part((1 - high) * 2, which * half, half),
+            weight_part(high * 2 + which, 0, columns),
+        ]
+
+    def weight_slots(row):
+        return [cross_weight.at[0, row], cross_weight.at[1, row], own_weight.at[row]]
 
     pairs = [
         (k_hbm, streams.at[1]),
@@ -116,10 +132,7 @@
         (inner_hbm, inner),
         (back_hbm, back),
         (last_hbm, last),
-        (block_of(1 - high, 1 - core), weight.at[0]),
-        (block_of(1 - high, core), weight.at[1]),
-        (block_of(high, 1 - core), weight.at[2]),
-        (block_of(high, core), weight.at[3]),
+        *zip(parts_for(core), weight_slots(0)),
     ]
     loads = [pltpu.make_async_copy(src, dst, load_sem.at[i]) for i, (src, dst) in enumerate(pairs)]
     for load in loads[:6]:
@@ -131,8 +144,8 @@
     def _(d):
         pl.semaphore_signal(barrier, inc=1, device_id=(lax.rem(me + d, n), chan), device_id_type=MESH)
 
-    pl.semaphore_signal(barrier, inc=1, device_id=(me, other_core), device_id_type=MESH)
-    pl.semaphore_signal(barrier, inc=1, device_id=(me, other_high), device_id_type=MESH)
+    for neighbour in (other_core, *across):
+        pl.semaphore_signal(barrier, inc=1, device_id=(me, neighbour), device_id_type=MESH)
     for load in loads[6:12]:
         load.start()
 
@@ -148,9 +161,9 @@
             ).start()
 
         place, depth = lax.div(me, DEPTH), lax.rem(me, DEPTH)
-        across, pair = lax.div(place, 2), lax.rem(place, 2)
+        row, pair = lax.div(place, 2), lax.rem(place, 2)
         for step_across, step_pair in ((2, 1), (2, 0), (1, 1), (3, 1), (1, 0), (3, 0), (0, 1), (0, 0)):
-            line = (lax.rem(across + step_across, n // DEPTH // 2) * 2 + lax.rem(pair + step_pair, 2)) * DEPTH
+            line = (lax.rem(row + step_across, n // DEPTH // 2) * 2 + lax.rem(pair + step_pair, 2)) * DEPTH
 
             @pl.loop(0, DEPTH if step_across + step_pair else DEPTH - 1)
             def _(i):
@@ -203,7 +216,7 @@
         tail[i * rim : (i + 1) * rim] = padded[i, edge + tokens - rim : edge + tokens]
     halo_out[...] = tail[...].astype(BF16)
 
-    pl.semaphore_wait(barrier, n + 1)
+    pl.semaphore_wait(barrier, n + 2)
     rims = pltpu.make_async_remote_copy(
         src_ref=halo_out,
         dst_ref=halo_in,
@@ -230,6 +243,19 @@
     exchange(send_p, recv_p, 1)
     for load in loads[12:]:
         load.start()
+    handed = []
+    for i, (src, dst) in enumerate(zip(parts_for(1 - core), weight_slots(1))):
+        handed.append(
+            pltpu.make_async_remote_copy(
+                src_ref=src,
+                dst_ref=dst,
+                send_sem=weight_send.at[i],
+                recv_sem=weight_recv.at[i],
+                device_id=(me, other_core),
+                device_id_type=MESH,
+            )
+        )
+        handed[-1].start()
     loads[5].wait()
     skipped[...] = skip[...] * product[...]
     q_short[...] = short(0, tokens)
@@ -270,62 +296,65 @@
 
     long_part = recv_y[...].astype(F32).reshape(channels, tokens)
     long_part = jnp.concatenate([long_part[i * tokens : (i + 1) * tokens].T for i in range(channels // tokens)], axis=1)
-    gated = (q_short[...] * (long_part + skipped[...])).astype(BF16)
-
-    width = columns // PARTS
-
-    def project(i, part):
-        return dot(gated, weight[i, :, part * width : (part + 1) * width])
-
-    def core_copy(half, part):
+    gated[0] = (q_short[...] * (long_part + skipped[...])).astype(BF16)
+    swap = pltpu.make_async_remote_copy(
+        src_ref=gated.at[0],
+        dst_ref=gated.at[1],
+        send_sem=gated_send,
+        recv_sem=gated_recv,
+        device_id=(me, other_core),
+        device_id_type=MESH,
+    )
+    swap.start()
+
+    width = half // PARTS
+
+    def cross_copy(target, part):
         return pltpu.make_async_remote_copy(
-            src_ref=send_core.at[half, part],
-            dst_ref=recv_core.at[half, part],
-            send_sem=core_send.at[half, part],
-            recv_sem=core_recv.at[half, part],
-            device_id=(me, other_core),
+            src_ref=send_cross.at[target, part],
+            dst_ref=recv_cross.at[core, part],
+            send_sem=cross_send.at[target, part],
+            recv_sem=cross_recv.at[core, part],
+            device_id=(me, across[target]),
             device_id_type=MESH,
         )
 
-    def cross_copy(part):
-        return pltpu.make_async_remote_copy(
-            src_ref=send_cross.at[part],
-            dst_ref=recv_cross.at[part],
-            send_sem=cross_send.at[part],
-            recv_sem=cross_recv.at[part],
-            device_id=(me, other_high),
-            device_id_type=MESH,
-        )
-
+    def cross_arrived(source, part):
+        pltpu.make_async_copy(recv_cross.at[source, part], recv_cross.at[source, part], cross_recv.at[source, part]).wait()
+
+    steps = [(target, part) for target in range(2) for part in range(PARTS)]
     for load in loads[12:]:
         load.wait()
-    kept = []
+
+    def project(row, target, part):
+        return dot(gated[row], cross_weight[target, row, :, part * width : (part + 1) * width])
+
+    for target, part in steps:
+        mine[target, part] = project(0, target, part)
+    for copy in handed:
+        copy.wait_recv()
+    swap.wait_recv()
+    for target, part in steps:
+        send_cross[target, part] = (mine[target, part] + project(1, target, part)).astype(BF16)
+        cross_copy(target, part).start()
+    for part in range(2 * PARTS):
+        span = slice(part * width, (part + 1) * width)
+        own[:, span] = dot(gated[0], own_weight[0, :, span]) + dot(gated[1], own_weight[1, :, span])
     for part in range(PARTS):
-        send_core[0, part] = project(0, part).astype(BF16)
-        core_copy(0, part).start()
-        kept.append(project(1, part))
-    for part in range(PARTS):
-        core_copy(0, part).wait_recv()
-        send_cross[part] = (kept[part] + recv_core[0, part].astype(F32)).astype(BF16)
-        cross_copy(part).start()
-    for part in range(PARTS):
-        send_core[1, part] = project(2, part).astype(BF16)
-        core_copy(1, part).start()
-    for part in range(PARTS):
-        mine = project(3, part)
-        core_copy(1, part).wait_recv()
-        mine = mine + recv_core[1, part].astype(F32)
-        cross_copy(part).wait_recv()
-        out_ref[:, part * width : (part + 1) * width] = (mine + recv_cross[part].astype(F32)).astype(BF16)
+        for source in range(2):
+            span = slice(source * half + part * width, source * half + (part + 1) * width)
+            cross_arrived(source, part)
+            out_ref[:, span] = (own[:, span] + recv_cross[source, part].astype(F32)).astype(BF16)
 
     rims.wait_send()
     left(send_h, 0)
     left(send_p, 1)
     left(send_y, 2)
-    for part in range(PARTS):
-        core_copy(0, part).wait_send()
-        core_copy(1, part).wait_send()
-        cross_copy(part).wait_send()
+    swap.wait_send()
+    for copy in handed:
+        copy.wait_send()
+    for target, part in steps:
+        cross_copy(target, part).wait_send()
 
 
 def body(n, q_stream, k_stream, v_stream, short_taps, long_filter, skip_gain, out_weight):
@@ -345,14 +374,15 @@
         out_weight,
         *tables,
     ]
-    width = columns // PARTS
+    width = columns // 2 // PARTS
     slabs = pltpu.VMEM((n, group, tokens), BF16)
     scratch = [
         pltpu.VMEM((3, tokens, channels), BF16),
         pltpu.VMEM(short_taps.shape, F32),
         pltpu.VMEM((tokens, channels), F32),
         pltpu.VMEM((1, channels), F32),
-        pltpu.VMEM((4, rows, columns), BF16),
+        pltpu.VMEM((2, 2, rows, columns // 2), BF16),
+        pltpu.VMEM((2, rows, columns), BF16),
         *[pltpu.VMEM(table.shape, table.dtype) for table in tables],
         pltpu.VMEM((EDGE, channels), BF16),
         pltpu.VMEM((EDGE, channels), BF16),
@@ -364,19 +394,22 @@
         *[slabs] * 6,
         pltpu.VMEM((channels, 2 * tokens), F32),
         pltpu.VMEM((channels, tokens), F32),
+        pltpu.VMEM((2, tokens, channels), BF16),
+        pltpu.VMEM((2, PARTS, tokens, width), F32),
+        pltpu.VMEM((tokens, columns), F32),
         pltpu.VMEM((2, PARTS, tokens, width), BF16),
         pltpu.VMEM((2, PARTS, tokens, width), BF16),
-        pltpu.VMEM((PARTS, tokens, width), BF16),
-        pltpu.VMEM((PARTS, tokens, width), BF16),
         pltpu.SemaphoreType.DMA((16,)),
         pltpu.SemaphoreType.DMA,
         pltpu.SemaphoreType.DMA,
         pltpu.SemaphoreType.DMA((3,)),
         pltpu.SemaphoreType.DMA((3,)),
+        pltpu.SemaphoreType.DMA((3,)),
+        pltpu.SemaphoreType.DMA((3,)),
+        pltpu.SemaphoreType.DMA,
+        pltpu.SemaphoreType.DMA,
         pltpu.SemaphoreType.DMA((2, PARTS)),
         pltpu.SemaphoreType.DMA((2, PARTS)),
-        pltpu.SemaphoreType.DMA((PARTS,)),
-        pltpu.SemaphoreType.DMA((PARTS,)),
     ]
     return pl.pallas_call(
         functools.partial(kernel, n),

time: 41.8 us -> 39.3 us (0.940); the launches traced: 41.8 us -> 38.8 us
  Pallas kernels: 41 us -> 38.1 us
    pallas_call x1, Pallas kernels: 41 us -> 38.1 us  [body(): pl.pallas_call(functools.partial(kernel, n), out_shape=pltpu.VMEM((tokens...]
where the time goes in v3:
time: 39.3 us; the launch traced here: 38.8 us
  Pallas kernels  38.1 us (97%)
  local copies, waits for them, and re-layouts  0.71 us (2%)
    pallas_call x1, Pallas kernels, body(): pl.pallas_call(functools.partial(kernel, n), out_shape=pltpu.VMEM((tokens...  38.1 us

profile of v3, /device:TPU:1, one launch (start us, length us, event | category | flops | bytes accessed | tf_op | source)
XLA Modules:
  0.0 38.8 jit_solution(47533755681482694)
XLA Ops:
  0.0 38.1 %shard_map.127 = bf16[128,1024]{1,0:T(8,128)(2,1)S(1)} custom-call(bf16[128,512]{1,0:T(8,128)(2,1)} %q_hbm.1, bf16[128,512]{1,0:T(8,128)(2,1)} %k_hbm.1, bf16[128,512]{1,0:T(8,128)(2,1)} %v_hbm.1, f32[3,3,512]{2,1,0:T(4,128)} %taps_hbm.1, f32[128,512]{1,0:T(8,128)} %filter_hbm.1, f32[1,512]{1,0:T(1,128)} %bitcast.1, bf16[512,4096]{1,0:T(8,128)(2,1)} %weight_hbm.1, ...), custom_call_target="tpu_custom_call" | custom-call | tf_op jit(solution)/shard_map/pallas_call | solution.py:414
  38.1 0.7 %copy.15 = bf16[128,1024]{1,0:T(8,128)(2,1)} copy(bf16[128,1024]{1,0:T(8,128)(2,1)S(1)} %shard_map.127) | data formatting | bytes 524288

commit v4 on v3

--- a/solution.py
+++ b/solution.py
@@ -67,6 +67,8 @@
     halo_out,
     halo_in,
     tail,
+    edge_out,
+    edge_in,
     padded,
     product,
     q_short,
@@ -95,6 +97,7 @@
     gated_recv,
     cross_send,
     cross_recv,
+    turn_sem,
 ):
     me, chan = lax.axis_index("seq"), lax.axis_index("chan")
     core, high = lax.rem(chan, 2), lax.div(chan, 2)
@@ -149,29 +152,37 @@
     for load in loads[6:12]:
         load.start()
 
-    def exchange(source, target, index):
+    def exchange(*routes):
         def send(peer):
-            pltpu.make_async_remote_copy(
-                src_ref=source.at[peer],
-                dst_ref=target.at[me],
-                send_sem=all_send.at[index],
-                recv_sem=all_recv.at[index],
-                device_id=(peer, chan),
-                device_id_type=MESH,
-            ).start()
+            for source, target, index in routes:
+                pltpu.make_async_remote_copy(
+                    src_ref=source(peer),
+                    dst_ref=target(me),
+                    send_sem=all_send.at[index],
+                    recv_sem=all_recv.at[index],
+                    device_id=(peer, chan),
+                    device_id_type=MESH,
+                ).start()
 
         place, depth = lax.div(me, DEPTH), lax.rem(me, DEPTH)
         row, pair = lax.div(place, 2), lax.rem(place, 2)
-        for step_across, step_pair in ((2, 1), (2, 0), (1, 1), (3, 1), (1, 0), (3, 0), (0, 1), (0, 0)):
-            line = (lax.rem(row + step_across, n // DEPTH // 2) * 2 + lax.rem(pair + step_pair, 2)) * DEPTH
-
-            @pl.loop(0, DEPTH if step_across + step_pair else DEPTH - 1)
+        for step_row, step_pair in ((2, 1), (2, 0), (1, 1), (3, 1), (1, 0), (3, 0), (0, 1), (0, 0)):
+            line = (lax.rem(row + step_row, n // DEPTH // 2) * 2 + lax.rem(pair + step_pair, 2)) * DEPTH
+
+            @pl.loop(0, DEPTH if step_row + step_pair else DEPTH - 1)
             def _(i):
                 far = DEPTH // 2 - lax.div(i + 1, 2)
                 step = jnp.where(lax.rem(i, 2) == 1, far, DEPTH - far)
                 send(line + lax.rem(depth + step, DEPTH))
 
-        target[me] = source[me]
+    def slabs(source, target, index):
+        return (lambda peer: source.at[peer], lambda own_place: target.at[own_place], index)
+
+    edges = (
+        lambda peer: edge_out.at[pl.ds(peer, 1)],
+        lambda own_place: edge_in.at[pl.ds(edge + own_place, 1)],
+        3,
+    )
 
     def arrived(buffer, index):
         part = buffer.at[pl.ds(0, n - 1)]
@@ -189,28 +200,39 @@
 
     edge = EDGE
 
-    def short(i, rows):
-        total = taps[i, 0:1] * padded[i, edge : edge + rows]
+    def short(i, first_row, rows):
+        start = edge + first_row
+        total = taps[i, 0:1] * padded[i, start : start + rows]
         for lag in range(1, taps.shape[1]):
-            total += taps[i, lag : lag + 1] * padded[i, edge - lag : edge - lag + rows]
+            total += taps[i, lag : lag + 1] * padded[i, start - lag : start - lag + rows]
         return total
 
     def fill(i):
         padded[i, 0:edge] = jnp.zeros((edge, channels), F32)
         padded[i, edge : edge + tokens] = streams[i].astype(F32)
+        padded[i, edge + tokens :] = jnp.zeros((edge, channels), F32)
 
     for load in loads[0:3]:
         load.wait()
     fill(1)
     fill(2)
-    product[...] = short(1, tokens) * short(2, tokens)
+    k_short, v_short = short(1, 0, tokens), short(2, 0, tokens)
+    product[...] = k_short * v_short
     to_channels(product[...], send_p)
+    rim = taps.shape[1] - 1
+    for i, value in enumerate((k_short, v_short, short(1, tokens, edge), short(2, tokens, edge))):
+        tail[i * rim : (i + 1) * rim] = value[:rim]
+    for i in range(channels // tokens):
+        flat[i * tokens : (i + 1) * tokens, 0:edge] = tail[:, i * tokens : (i + 1) * tokens].T
+    pieces = [flat[pl.ds(c, n, stride=group)][:, 0:edge] for c in range(group)]
+    edge_out[:, 0 : group * edge] = jnp.concatenate(pieces, axis=1)
+    edge_out[:, group * edge :] = jnp.zeros((n, tokens - group * edge), F32)
+    edge_in[0:edge] = jnp.zeros((edge, tokens), F32)
     loads[3].wait()
     to_channels(filt[...], send_h)
     loads[4].wait()
     fill(0)
 
-    rim = taps.shape[1] - 1
     tail[...] = jnp.zeros(tail.shape, F32)
     for i in range(3):
         tail[i * rim : (i + 1) * rim] = padded[i, edge + tokens - rim : edge + tokens]
@@ -225,22 +247,23 @@
         device_id=(lax.rem(me + 1, n), chan),
         device_id_type=MESH,
     )
+    exchange(slabs(send_h, recv_h, 0))
+
+    @pl.when(core == 1)
+    def _():
+        pl.semaphore_wait(turn_sem, 1)
+
+    exchange(slabs(send_p, recv_p, 1), edges)
+
+    @pl.when(core == 0)
+    def _():
+        left(send_h, 0)
+        pl.semaphore_signal(turn_sem, inc=1, device_id=(me, other_core), device_id_type=MESH)
+
     rims.start()
-    exchange(send_h, recv_h, 0)
-
-    inside = jnp.where(me > 0, 1.0, 0.0).astype(F32)
-
-    rims.wait_recv()
-    tail[...] = halo_in[...].astype(F32) * inside
-    for i in range(3):
-        padded[i, edge - rim : edge] = tail[i * rim : (i + 1) * rim]
-    head = short(1, edge) * short(2, edge)
-    product[0:edge] = head
-    for i in range(channels // tokens):
-        per = tokens // group
-        turned = head[:, i * tokens : (i + 1) * tokens].T.reshape(per, group, edge).astype(BF16)
-        send_p[i * per : (i + 1) * per, :, 0:edge] = turned
-    exchange(send_p, recv_p, 1)
+    recv_h[me] = send_h[me]
+    recv_p[me] = send_p[me]
+    edge_in[pl.ds(edge + me, 1)] = edge_out[pl.ds(me, 1)]
     for load in loads[12:]:
         load.start()
     handed = []
@@ -256,16 +279,17 @@
             )
         )
         handed[-1].start()
-    loads[5].wait()
-    skipped[...] = skip[...] * product[...]
-    q_short[...] = short(0, tokens)
-
     for load in loads[6:12]:
         load.wait()
 
-    def forward(buffer):
+    def forward(buffer, heads=None):
         flat[...] = buffer[...].astype(F32).reshape(channels, tokens)
-        signal = [flat[pl.ds(c, n, stride=group)].astype(BF16) for c in range(group)]
+        signal = [flat[pl.ds(c, n, stride=group)] for c in range(group)]
+        if heads is not None:
+            first_lanes = lax.broadcasted_iota(jnp.int32, (n, tokens), 1) < rim
+            moved = [pltpu.roll(heads, (tokens - c * edge) % tokens, axis=1) for c in range(group)]
+            signal = [jnp.where(first_lanes, new, old) for new, old in zip(moved, signal)]
+        signal = [value.astype(BF16) for value in signal]
         stage = dot(first[...], jnp.concatenate(signal, axis=1))
         turned = []
         for c in range(group):
@@ -277,7 +301,11 @@
     arrived(recv_h, 0)
     response[...] = forward(recv_h)
     arrived(recv_p, 1)
-    spectrum = forward(recv_p)
+    pltpu.make_async_copy(edge_in.at[pl.ds(0, n - 1)], edge_in.at[pl.ds(0, n - 1)], all_recv.at[3]).wait()
+    before = pltpu.roll(edge_in[edge - 1 : edge - 1 + n], tokens - 2 * rim, axis=1)
+    completed = edge_in[edge : edge + n] + before
+    heads = completed * pltpu.roll(completed, tokens - rim, axis=1)
+    spectrum = forward(recv_p, heads)
     p_real, p_imag = spectrum[:, :tokens], spectrum[:, tokens:]
     h_real, h_imag = response[:, :tokens], response[:, tokens:]
     filtered = [p_real * h_real - p_imag * h_imag, p_real * h_imag + p_imag * h_real]
@@ -291,7 +319,17 @@
     for c in range(group):
         flat[pl.ds(c, n, stride=group)] = convolved[:, c * tokens : (c + 1) * tokens]
     send_y[...] = flat[...].reshape(n, group, tokens).astype(BF16)
-    exchange(send_y, recv_y, 2)
+    exchange(slabs(send_y, recv_y, 2))
+    recv_y[me] = send_y[me]
+    loads[5].wait()
+    rims.wait_recv()
+    inside = jnp.where(me > 0, 1.0, 0.0).astype(F32)
+    tail[...] = halo_in[...].astype(F32) * inside
+    for i in range(3):
+        padded[i, edge - rim : edge] = tail[i * rim : (i + 1) * rim]
+    product[0:edge] = short(1, 0, edge) * short(2, 0, edge)
+    skipped[...] = skip[...] * product[...]
+    q_short[...] = short(0, 0, tokens)
     arrived(recv_y, 2)
 
     long_part = recv_y[...].astype(F32).reshape(channels, tokens)
@@ -347,9 +385,10 @@
             out_ref[:, span] = (own[:, span] + recv_cross[source, part].astype(F32)).astype(BF16)
 
     rims.wait_send()
-    left(send_h, 0)
+    pl.when(core == 1)(lambda: left(send_h, 0))
     left(send_p, 1)
     left(send_y, 2)
+    pltpu.make_async_copy(edge_out.at[pl.ds(0, n - 1)], edge_out.at[pl.ds(0, n - 1)], all_send.at[3]).wait()
     swap.wait_send()
     for copy in handed:
         copy.wait_send()
@@ -387,7 +426,9 @@
         pltpu.VMEM((EDGE, channels), BF16),
         pltpu.VMEM((EDGE, channels), BF16),
         pltpu.VMEM((EDGE, channels), F32),
-        pltpu.VMEM((3, EDGE + tokens, channels), F32),
+        pltpu.VMEM((n, tokens), F32),
+        pltpu.VMEM((EDGE + n, tokens), F32),
+        pltpu.VMEM((3, 2 * EDGE + tokens, channels), F32),
         pltpu.VMEM((tokens, channels), F32),
         pltpu.VMEM((tokens, channels), F32),
         pltpu.VMEM((tokens, channels), F32),
@@ -402,14 +443,15 @@
         pltpu.SemaphoreType.DMA((16,)),
         pltpu.SemaphoreType.DMA,
         pltpu.SemaphoreType.DMA,
-        pltpu.SemaphoreType.DMA((3,)),
-        pltpu.SemaphoreType.DMA((3,)),
+        pltpu.SemaphoreType.DMA((4,)),
+        pltpu.SemaphoreType.DMA((4,)),
         pltpu.SemaphoreType.DMA((3,)),
         pltpu.SemaphoreType.DMA((3,)),
         pltpu.SemaphoreType.DMA,
         pltpu.SemaphoreType.DMA,
         pltpu.SemaphoreType.DMA((2, PARTS)),
         pltpu.SemaphoreType.DMA((2, PARTS)),
+        pltpu.SemaphoreType.REGULAR,
     ]
     return pl.pallas_call(
         functools.partial(kernel, n),

time: 39.3 us -> 38.7 us (0.985); the launches traced: 38.8 us -> 38.6 us
  no operation moved by 1% of the time
where the time goes in v4:
time: 38.7 us; the launch traced here: 38.6 us
  Pallas kernels  37.9 us (98%)
  local copies, waits for them, and re-layouts  0.71 us (2%)
    pallas_call x1, Pallas kernels, body(): pl.pallas_call(functools.partial(kernel, n), out_shape=pltpu.VMEM((tokens...  37.9 us

profile of v4, /device:TPU:1, one launch (start us, length us, event | category | flops | bytes accessed | tf_op | source)
XLA Modules:
  0.0 38.6 jit_solution(17503015731645019681)
XLA Ops:
  0.0 37.9 %shard_map.127 = bf16[128,1024]{1,0:T(8,128)(2,1)S(1)} custom-call(bf16[128,512]{1,0:T(8,128)(2,1)} %q_hbm.1, bf16[128,512]{1,0:T(8,128)(2,1)} %k_hbm.1, bf16[128,512]{1,0:T(8,128)(2,1)} %v_hbm.1, f32[3,3,512]{2,1,0:T(4,128)} %taps_hbm.1, f32[128,512]{1,0:T(8,128)} %filter_hbm.1, f32[1,512]{1,0:T(1,128)} %bitcast.1, bf16[512,4096]{1,0:T(8,128)(2,1)} %weight_hbm.1, ...), custom_call_target="tpu_custom_call" | custom-call | tf_op jit(solution)/shard_map/pallas_call | solution.py:456
  37.9 0.7 %copy.15 = bf16[128,1024]{1,0:T(8,128)(2,1)} copy(bf16[128,1024]{1,0:T(8,128)(2,1)S(1)} %shard_map.127) | data formatting | bytes 524288

commit v5 on v4

--- a/solution.py
+++ b/solution.py
@@ -73,13 +73,10 @@
     product,
     q_short,
     skipped,
-    send_h,
-    send_p,
+    send_both,
+    recv_both,
     send_y,
-    recv_h,
-    recv_p,
     recv_y,
-    response,
     flat,
     gated,
     mine,
@@ -97,7 +94,6 @@
     gated_recv,
     cross_send,
     cross_recv,
-    turn_sem,
 ):
     me, chan = lax.axis_index("seq"), lax.axis_index("chan")
     core, high = lax.rem(chan, 2), lax.div(chan, 2)
@@ -141,12 +137,24 @@
     for load in loads[:6]:
         load.start()
 
+    def rounds(send):
+        place, depth = lax.div(me, DEPTH), lax.rem(me, DEPTH)
+        row, pair = lax.div(place, 2), lax.rem(place, 2)
+        for step_row, step_pair in ((2, 1), (2, 0), (1, 1), (3, 1), (1, 0), (3, 0), (0, 1), (0, 0)):
+            line = (lax.rem(row + step_row, n // DEPTH // 2) * 2 + lax.rem(pair + step_pair, 2)) * DEPTH
+
+            @pl.loop(0, DEPTH if step_row + step_pair else DEPTH - 1)
+            def _(i):
+                far = DEPTH // 2 - lax.div(i + 1, 2)
+                step = jnp.where(lax.rem(i, 2) == 1, far, DEPTH - far)
+                send(line + lax.rem(depth + step, DEPTH))
+
     barrier = pltpu.get_barrier_semaphore()
 
-    @pl.loop(1, n)
-    def _(d):
-        pl.semaphore_signal(barrier, inc=1, device_id=(lax.rem(me + d, n), chan), device_id_type=MESH)
-
+    def greet(peer):
+        pl.semaphore_signal(barrier, inc=1, device_id=(peer, chan), device_id_type=MESH)
+
+    rounds(greet)
     for neighbour in (other_core, *across):
         pl.semaphore_signal(barrier, inc=1, device_id=(me, neighbour), device_id_type=MESH)
     for load in loads[6:12]:
@@ -164,16 +172,7 @@
                     device_id_type=MESH,
                 ).start()
 
-        place, depth = lax.div(me, DEPTH), lax.rem(me, DEPTH)
-        row, pair = lax.div(place, 2), lax.rem(place, 2)
-        for step_row, step_pair in ((2, 1), (2, 0), (1, 1), (3, 1), (1, 0), (3, 0), (0, 1), (0, 0)):
-            line = (lax.rem(row + step_row, n // DEPTH // 2) * 2 + lax.rem(pair + step_pair, 2)) * DEPTH
-
-            @pl.loop(0, DEPTH if step_row + step_pair else DEPTH - 1)
-            def _(i):
-                far = DEPTH // 2 - lax.div(i + 1, 2)
-                step = jnp.where(lax.rem(i, 2) == 1, far, DEPTH - far)
-                send(line + lax.rem(depth + step, DEPTH))
+        rounds(send)
 
     def slabs(source, target, index):
         return (lambda peer: source.at[peer], lambda own_place: target.at[own_place], index)
@@ -181,7 +180,7 @@
     edges = (
         lambda peer: edge_out.at[pl.ds(peer, 1)],
         lambda own_place: edge_in.at[pl.ds(edge + own_place, 1)],
-        3,
+        1,
     )
 
     def arrived(buffer, index):
@@ -191,12 +190,6 @@
     def left(buffer, index):
         part = buffer.at[pl.ds(0, n - 1)]
         pltpu.make_async_copy(part, part, all_send.at[index]).wait()
-
-    def to_channels(value, buffer):
-        per = tokens // group
-        for i in range(channels // tokens):
-            turned = value[:, i * tokens : (i + 1) * tokens].T
-            buffer[i * per : (i + 1) * per] = turned.reshape(per, group, tokens).astype(BF16)
 
     edge = EDGE
 
@@ -218,18 +211,20 @@
     fill(2)
     k_short, v_short = short(1, 0, tokens), short(2, 0, tokens)
     product[...] = k_short * v_short
-    to_channels(product[...], send_p)
     rim = taps.shape[1] - 1
     for i, value in enumerate((k_short, v_short, short(1, tokens, edge), short(2, tokens, edge))):
         tail[i * rim : (i + 1) * rim] = value[:rim]
     for i in range(channels // tokens):
-        flat[i * tokens : (i + 1) * tokens, 0:edge] = tail[:, i * tokens : (i + 1) * tokens].T
-    pieces = [flat[pl.ds(c, n, stride=group)][:, 0:edge] for c in range(group)]
+        flat[0, i * tokens : (i + 1) * tokens, 0:edge] = tail[:, i * tokens : (i + 1) * tokens].T
+    pieces = [flat[0, pl.ds(c, n, stride=group)][:, 0:edge] for c in range(group)]
     edge_out[:, 0 : group * edge] = jnp.concatenate(pieces, axis=1)
     edge_out[:, group * edge :] = jnp.zeros((n, tokens - group * edge), F32)
     edge_in[0:edge] = jnp.zeros((edge, tokens), F32)
     loads[3].wait()
-    to_channels(filt[...], send_h)
+    per = tokens // group
+    for i in range(channels // tokens):
+        both = [value[:, i * tokens : (i + 1) * tokens].T.reshape(per, group, tokens) for value in (filt, product)]
+        send_both[i * per : (i + 1) * per] = jnp.concatenate(both, axis=1).astype(BF16)
     loads[4].wait()
     fill(0)
 
@@ -247,22 +242,9 @@
         device_id=(lax.rem(me + 1, n), chan),
         device_id_type=MESH,
     )
-    exchange(slabs(send_h, recv_h, 0))
-
-    @pl.when(core == 1)
-    def _():
-        pl.semaphore_wait(turn_sem, 1)
-
-    exchange(slabs(send_p, recv_p, 1), edges)
-
-    @pl.when(core == 0)
-    def _():
-        left(send_h, 0)
-        pl.semaphore_signal(turn_sem, inc=1, device_id=(me, other_core), device_id_type=MESH)
-
+    exchange(slabs(send_both, recv_both, 0), edges)
     rims.start()
-    recv_h[me] = send_h[me]
-    recv_p[me] = send_p[me]
+    recv_both[me] = send_both[me]
     edge_in[pl.ds(edge + me, 1)] = edge_out[pl.ds(me, 1)]
     for load in loads[12:]:
         load.start()
@@ -282,9 +264,10 @@
     for load in loads[6:12]:
         load.wait()
 
-    def forward(buffer, heads=None):
-        flat[...] = buffer[...].astype(F32).reshape(channels, tokens)
-        signal = [flat[pl.ds(c, n, stride=group)] for c in range(group)]
+    def forward(which, heads=None):
+        slab = recv_both[...].astype(F32)[:, which * group : (which + 1) * group]
+        flat[which] = slab.reshape(channels, tokens)
+        signal = [flat[which, pl.ds(c, n, stride=group)] for c in range(group)]
         if heads is not None:
             first_lanes = lax.broadcasted_iota(jnp.int32, (n, tokens), 1) < rim
             moved = [pltpu.roll(heads, (tokens - c * edge) % tokens, axis=1) for c in range(group)]
@@ -298,14 +281,13 @@
             turned.append(jnp.concatenate(pair, axis=1).astype(BF16))
         return dot(jnp.concatenate(turned, axis=0), inner[...])
 
-    arrived(recv_h, 0)
-    response[...] = forward(recv_h)
-    arrived(recv_p, 1)
-    pltpu.make_async_copy(edge_in.at[pl.ds(0, n - 1)], edge_in.at[pl.ds(0, n - 1)], all_recv.at[3]).wait()
+    arrived(recv_both, 0)
+    pltpu.make_async_copy(edge_in.at[pl.ds(0, n - 1)], edge_in.at[pl.ds(0, n - 1)], all_recv.at[1]).wait()
     before = pltpu.roll(edge_in[edge - 1 : edge - 1 + n], tokens - 2 * rim, axis=1)
     completed = edge_in[edge : edge + n] + before
     heads = completed * pltpu.roll(completed, tokens - rim, axis=1)
-    spectrum = forward(recv_p, heads)
+    response = forward(0)
+    spectrum = forward(1, heads)
     p_real, p_imag = spectrum[:, :tokens], spectrum[:, tokens:]
     h_real, h_imag = response[:, :tokens], response[:, tokens:]
     filtered = [p_real * h_real - p_imag * h_imag, p_real * h_imag + p_imag * h_real]
@@ -317,8 +299,8 @@
         turned.append(jnp.concatenate(pair, axis=0).astype(BF16))
     convolved = dot(last[...], jnp.concatenate(turned, axis=1))
     for c in range(group):
-        flat[pl.ds(c, n, stride=group)] = convolved[:, c * tokens : (c + 1) * tokens]
-    send_y[...] = flat[...].reshape(n, group, tokens).astype(BF16)
+        flat[0, pl.ds(c, n, stride=group)] = convolved[:, c * tokens : (c + 1) * tokens]
+    send_y[...] = flat[0].reshape(n, group, tokens).astype(BF16)
     exchange(slabs(send_y, recv_y, 2))
     recv_y[me] = send_y[me]
     loads[5].wait()
@@ -367,13 +349,14 @@
     def project(row, target, part):
         return dot(gated[row], cross_weight[target, row, :, part * width : (part + 1) * width])
 
-    for target, part in steps:
-        mine[target, part] = project(0, target, part)
+    lead = steps[0]
+    mine[lead] = project(0, *lead)
     for copy in handed:
         copy.wait_recv()
     swap.wait_recv()
     for target, part in steps:
-        send_cross[target, part] = (mine[target, part] + project(1, target, part)).astype(BF16)
+        early = mine[lead] if (target, part) == lead else project(0, target, part)
+        send_cross[target, part] = (early + project(1, target, part)).astype(BF16)
         cross_copy(target, part).start()
     for part in range(2 * PARTS):
         span = slice(part * width, (part + 1) * width)
@@ -385,10 +368,9 @@
             out_ref[:, span] = (own[:, span] + recv_cross[source, part].astype(F32)).astype(BF16)
 
     rims.wait_send()
-    pl.when(core == 1)(lambda: left(send_h, 0))
-    left(send_p, 1)
+    left(send_both, 0)
     left(send_y, 2)
-    pltpu.make_async_copy(edge_out.at[pl.ds(0, n - 1)], edge_out.at[pl.ds(0, n - 1)], all_send.at[3]).wait()
+    pltpu.make_async_copy(edge_out.at[pl.ds(0, n - 1)], edge_out.at[pl.ds(0, n - 1)], all_send.at[1]).wait()
     swap.wait_send()
     for copy in handed:
         copy.wait_send()
@@ -432,9 +414,9 @@
         pltpu.VMEM((tokens, channels), F32),
         pltpu.VMEM((tokens, channels), F32),
         pltpu.VMEM((tokens, channels), F32),
-        *[slabs] * 6,
-        pltpu.VMEM((channels, 2 * tokens), F32),
-        pltpu.VMEM((channels, tokens), F32),
+        *[pltpu.VMEM((n, 2 * group, tokens), BF16)] * 2,
+        *[slabs] * 2,
+        pltpu.VMEM((2, channels, tokens), F32),
         pltpu.VMEM((2, tokens, channels), BF16),
         pltpu.VMEM((2, PARTS, tokens, width), F32),
         pltpu.VMEM((tokens, columns), F32),
@@ -443,15 +425,14 @@
         pltpu.SemaphoreType.DMA((16,)),
         pltpu.SemaphoreType.DMA,
         pltpu.SemaphoreType.DMA,
-        pltpu.SemaphoreType.DMA((4,)),
-        pltpu.SemaphoreType.DMA((4,)),
+        pltpu.SemaphoreType.DMA((3,)),
+        pltpu.SemaphoreType.DMA((3,)),
         pltpu.SemaphoreType.DMA((3,)),
         pltpu.SemaphoreType.DMA((3,)),
         pltpu.SemaphoreType.DMA,
         pltpu.SemaphoreType.DMA,
         pltpu.SemaphoreType.DMA((2, PARTS)),
         pltpu.SemaphoreType.DMA((2, PARTS)),
-        pltpu.SemaphoreType.REGULAR,
     ]
     return pl.pallas_call(
         functools.partial(kernel, n),

time: 38.7 us -> 38.3 us (0.990)
  Pallas kernels: 37.9 us -> 37.1 us
    pallas_call x1, Pallas kernels: 37.9 us -> 37.1 us  [body(): pl.pallas_call(functools.partial(kernel, n), out_shape=pltpu.VMEM((tokens...]
where the time goes in v5:
time: 38.3 us; the launch traced here: 37.8 us
  Pallas kernels  37.1 us (97%)
  local copies, waits for them, and re-layouts  0.71 us (2%)
    pallas_call x1, Pallas kernels, body(): pl.pallas_call(functools.partial(kernel, n), out_shape=pltpu.VMEM((tokens...  37.1 us

profile of v5, /device:TPU:1, one launch (start us, length us, event | category | flops | bytes accessed | tf_op | source)
XLA Modules:
  0.0 37.8 jit_solution(10385271104919270656)
XLA Ops:
  0.0 37.1 %shard_map.127 = bf16[128,1024]{1,0:T(8,128)(2,1)S(1)} custom-call(bf16[128,512]{1,0:T(8,128)(2,1)} %q_hbm.1, bf16[128,512]{1,0:T(8,128)(2,1)} %k_hbm.1, bf16[128,512]{1,0:T(8,128)(2,1)} %v_hbm.1, f32[3,3,512]{2,1,0:T(4,128)} %taps_hbm.1, f32[128,512]{1,0:T(8,128)} %filter_hbm.1, f32[1,512]{1,0:T(1,128)} %bitcast.1, bf16[512,4096]{1,0:T(8,128)(2,1)} %weight_hbm.1, ...), custom_call_target="tpu_custom_call" | custom-call | tf_op jit(solution)/shard_map/pallas_call | solution.py:437
  37.1 0.7 %copy.15 = bf16[128,1024]{1,0:T(8,128)(2,1)} copy(bf16[128,1024]{1,0:T(8,128)(2,1)S(1)} %shard_map.127) | data formatting | bytes 524288

commit v6 on v5

--- a/solution.py
+++ b/solution.py
@@ -16,6 +16,20 @@
 EDGE = 8
 PARTS = 2
 DEPTH = 8
+SPLIT = 2
+
+
+def narrow(table):
+    return table.astype(ml_dtypes.bfloat16)
+
+
+def in_two(table, axis):
+    high = narrow(table)
+    return np.concatenate([high, narrow(table - high.astype(np.float64))], axis=axis)
+
+
+def twice(value, axis):
+    return jnp.concatenate([value, value], axis=axis)
 
 
 def transform_tables(blocks, tokens):
@@ -28,7 +42,7 @@
     cosine, sine = np.cos(inner_angle), np.sin(inner_angle)
     inner = np.block([[cosine, sine], [-sine, cosine]])
     back = np.block([[cosine, -sine], [sine, cosine]]) / length
-    matrices = [table.astype(ml_dtypes.bfloat16) for table in (outer, outer.T.copy(), inner, back)]
+    matrices = [in_two(outer, 1), in_two(outer.T, 1), narrow(inner), narrow(back)]
     return (*matrices, np.cos(turn).astype(np.float32), np.sin(turn).astype(np.float32))
 
 
@@ -94,6 +108,7 @@
     gated_recv,
     cross_send,
     cross_recv,
+    turn_sem,
 ):
     me, chan = lax.axis_index("seq"), lax.axis_index("chan")
     core, high = lax.rem(chan, 2), lax.div(chan, 2)
@@ -137,10 +152,12 @@
     for load in loads[:6]:
         load.start()
 
-    def rounds(send):
+    lines = ((2, 1), (2, 0), (1, 1), (3, 1), (1, 0), (3, 0), (0, 1), (0, 0))
+
+    def rounds(send, chosen=lines):
         place, depth = lax.div(me, DEPTH), lax.rem(me, DEPTH)
         row, pair = lax.div(place, 2), lax.rem(place, 2)
-        for step_row, step_pair in ((2, 1), (2, 0), (1, 1), (3, 1), (1, 0), (3, 0), (0, 1), (0, 0)):
+        for step_row, step_pair in chosen:
             line = (lax.rem(row + step_row, n // DEPTH // 2) * 2 + lax.rem(pair + step_pair, 2)) * DEPTH
 
             @pl.loop(0, DEPTH if step_row + step_pair else DEPTH - 1)
@@ -160,35 +177,36 @@
     for load in loads[6:12]:
         load.start()
 
-    def exchange(*routes):
+    def exchange(*routes, chosen=lines):
         def send(peer):
-            for source, target, index in routes:
+            for source, target, index, leaves in routes:
                 pltpu.make_async_remote_copy(
                     src_ref=source(peer),
                     dst_ref=target(me),
-                    send_sem=all_send.at[index],
+                    send_sem=all_send.at[leaves],
                     recv_sem=all_recv.at[index],
                     device_id=(peer, chan),
                     device_id_type=MESH,
                 ).start()
 
-        rounds(send)
-
-    def slabs(source, target, index):
-        return (lambda peer: source.at[peer], lambda own_place: target.at[own_place], index)
+        rounds(send, chosen)
+
+    def slabs(source, target, index, leaves):
+        return (lambda peer: source.at[peer], lambda own_place: target.at[own_place], index, leaves)
 
     edges = (
         lambda peer: edge_out.at[pl.ds(peer, 1)],
         lambda own_place: edge_in.at[pl.ds(edge + own_place, 1)],
         1,
+        1,
     )
 
     def arrived(buffer, index):
         part = buffer.at[pl.ds(0, n - 1)]
         pltpu.make_async_copy(part, part, all_recv.at[index]).wait()
 
-    def left(buffer, index):
-        part = buffer.at[pl.ds(0, n - 1)]
+    def left(buffer, index, count):
+        part = buffer.at[pl.ds(0, count)]
         pltpu.make_async_copy(part, part, all_send.at[index]).wait()
 
     edge = EDGE
@@ -242,7 +260,19 @@
         device_id=(lax.rem(me + 1, n), chan),
         device_id_type=MESH,
     )
-    exchange(slabs(send_both, recv_both, 0), edges)
+    exchange(slabs(send_both, recv_both, 0, 0), edges, chosen=lines[:SPLIT])
+
+    @pl.when(core == 1)
+    def _():
+        pl.semaphore_wait(turn_sem, 1)
+
+    exchange(slabs(send_both, recv_both, 0, 3), edges, chosen=lines[SPLIT:])
+
+    @pl.when(core == 0)
+    def _():
+        left(send_both, 0, SPLIT * DEPTH)
+        pl.semaphore_signal(turn_sem, inc=1, device_id=(me, other_core), device_id_type=MESH)
+
     rims.start()
     recv_both[me] = send_both[me]
     edge_in[pl.ds(edge + me, 1)] = edge_out[pl.ds(me, 1)]
@@ -273,7 +303,7 @@
             moved = [pltpu.roll(heads, (tokens - c * edge) % tokens, axis=1) for c in range(group)]
             signal = [jnp.where(first_lanes, new, old) for new, old in zip(moved, signal)]
         signal = [value.astype(BF16) for value in signal]
-        stage = dot(first[...], jnp.concatenate(signal, axis=1))
+        stage = dot(first[...], twice(jnp.concatenate(signal, axis=1), 0))
         turned = []
         for c in range(group):
             real, imag = stage[:n, c * tokens : (c + 1) * tokens], stage[n:, c * tokens : (c + 1) * tokens]
@@ -297,11 +327,11 @@
         real, imag = mixed[c * n : (c + 1) * n, :tokens], mixed[c * n : (c + 1) * n, tokens:]
         pair = [real * cosine[...] + imag * sine[...], imag * cosine[...] - real * sine[...]]
         turned.append(jnp.concatenate(pair, axis=0).astype(BF16))
-    convolved = dot(last[...], jnp.concatenate(turned, axis=1))
+    convolved = dot(last[...], twice(jnp.concatenate(turned, axis=1), 0))
     for c in range(group):
         flat[0, pl.ds(c, n, stride=group)] = convolved[:, c * tokens : (c + 1) * tokens]
     send_y[...] = flat[0].reshape(n, group, tokens).astype(BF16)
-    exchange(slabs(send_y, recv_y, 2))
+    exchange(slabs(send_y, recv_y, 2, 2))
     recv_y[me] = send_y[me]
     loads[5].wait()
     rims.wait_recv()
@@ -368,8 +398,9 @@
             out_ref[:, span] = (own[:, span] + recv_cross[source, part].astype(F32)).astype(BF16)
 
     rims.wait_send()
-    left(send_both, 0)
-    left(send_y, 2)
+    pl.when(core == 1)(lambda: left(send_both, 0, SPLIT * DEPTH))
+    left(send_both, 3, n - 1 - SPLIT * DEPTH)
+    left(send_y, 2, n - 1)
     pltpu.make_async_copy(edge_out.at[pl.ds(0, n - 1)], edge_out.at[pl.ds(0, n - 1)], all_send.at[1]).wait()
     swap.wait_send()
     for copy in handed:
@@ -425,7 +456,7 @@
         pltpu.SemaphoreType.DMA((16,)),
         pltpu.SemaphoreType.DMA,
         pltpu.SemaphoreType.DMA,
-        pltpu.SemaphoreType.DMA((3,)),
+        pltpu.SemaphoreType.DMA((4,)),
         pltpu.SemaphoreType.DMA((3,)),
         pltpu.SemaphoreType.DMA((3,)),
         pltpu.SemaphoreType.DMA((3,)),
@@ -433,6 +464,7 @@
         pltpu.SemaphoreType.DMA,
         pltpu.SemaphoreType.DMA((2, PARTS)),
         pltpu.SemaphoreType.DMA((2, PARTS)),
+        pltpu.SemaphoreType.REGULAR,
     ]
     return pl.pallas_call(
         functools.partial(kernel, n),

time: 38.3 us -> 38.1 us (level)
  no operation moved by 1% of the time
where the time goes in v6:
time: 38.1 us; the launch traced here: 37.8 us
  Pallas kernels  37.1 us (97%)
  local copies, waits for them, and re-layouts  0.71 us (2%)
    pallas_call x1, Pallas kernels, body(): pl.pallas_call(functools.partial(kernel, n), out_shape=pltpu.VMEM((tokens...  37.1 us

profile of v6, /device:TPU:1, one launch (start us, length us, event | category | flops | bytes accessed | tf_op | source)
XLA Modules:
  0.0 37.8 jit_solution(5638706147357339477)
XLA Ops:
  0.0 37.1 %shard_map.127 = bf16[128,1024]{1,0:T(8,128)(2,1)S(1)} custom-call(bf16[128,512]{1,0:T(8,128)(2,1)} %q_hbm.1, bf16[128,512]{1,0:T(8,128)(2,1)} %k_hbm.1, bf16[128,512]{1,0:T(8,128)(2,1)} %v_hbm.1, f32[3,3,512]{2,1,0:T(4,128)} %taps_hbm.1, f32[128,512]{1,0:T(8,128)} %filter_hbm.1, f32[1,512]{1,0:T(1,128)} %bitcast.1, bf16[512,4096]{1,0:T(8,128)(2,1)} %weight_hbm.1, ...), custom_call_target="tpu_custom_call" | custom-call | tf_op jit(solution)/shard_map/pallas_call | solution.py:469
  37.1 0.7 %copy.15 = bf16[128,1024]{1,0:T(8,128)(2,1)} copy(bf16[128,1024]{1,0:T(8,128)(2,1)S(1)} %shard_map.127) | data formatting | bytes 524288

commit v7 on v6

--- a/solution.py
+++ b/solution.py
@@ -345,17 +345,21 @@
     arrived(recv_y, 2)
 
     long_part = recv_y[...].astype(F32).reshape(channels, tokens)
-    long_part = jnp.concatenate([long_part[i * tokens : (i + 1) * tokens].T for i in range(channels // tokens)], axis=1)
-    gated[0] = (q_short[...] * (long_part + skipped[...])).astype(BF16)
-    swap = pltpu.make_async_remote_copy(
-        src_ref=gated.at[0],
-        dst_ref=gated.at[1],
-        send_sem=gated_send,
-        recv_sem=gated_recv,
-        device_id=(me, other_core),
-        device_id_type=MESH,
-    )
-    swap.start()
+    swaps = []
+    for i in range(channels // tokens):
+        span = slice(i * tokens, (i + 1) * tokens)
+        gated[0, :, span] = (q_short[:, span] * (long_part[span].T + skipped[:, span])).astype(BF16)
+        swaps.append(
+            pltpu.make_async_remote_copy(
+                src_ref=gated.at[0, :, pl.ds(i * tokens, tokens)],
+                dst_ref=gated.at[1, :, pl.ds(i * tokens, tokens)],
+                send_sem=gated_send.at[i],
+                recv_sem=gated_recv.at[i],
+                device_id=(me, other_core),
+                device_id_type=MESH,
+            )
+        )
+        swaps[-1].start()
 
     width = half // PARTS
 
@@ -383,7 +387,8 @@
     mine[lead] = project(0, *lead)
     for copy in handed:
         copy.wait_recv()
-    swap.wait_recv()
+    for swap in swaps:
+        swap.wait_recv()
     for target, part in steps:
         early = mine[lead] if (target, part) == lead else project(0, target, part)
         send_cross[target, part] = (early + project(1, target, part)).astype(BF16)
@@ -402,7 +407,8 @@
     left(send_both, 3, n - 1 - SPLIT * DEPTH)
     left(send_y, 2, n - 1)
     pltpu.make_async_copy(edge_out.at[pl.ds(0, n - 1)], edge_out.at[pl.ds(0, n - 1)], all_send.at[1]).wait()
-    swap.wait_send()
+    for swap in swaps:
+        swap.wait_send()
     for copy in handed:
         copy.wait_send()
     for target, part in steps:
@@ -460,8 +466,8 @@
         pltpu.SemaphoreType.DMA((3,)),
         pltpu.SemaphoreType.DMA((3,)),
         pltpu.SemaphoreType.DMA((3,)),
-        pltpu.SemaphoreType.DMA,
-        pltpu.SemaphoreType.DMA,
+        pltpu.SemaphoreType.DMA((channels // tokens,)),
+        pltpu.SemaphoreType.DMA((channels // tokens,)),
         pltpu.SemaphoreType.DMA((2, PARTS)),
         pltpu.SemaphoreType.DMA((2, PARTS)),
         pltpu.SemaphoreType.REGULAR,

time: 38.1 us -> 38.1 us (level)
  no operation moved by 1% of the time
where the time goes in v7:
time: 38.1 us; the launch traced here: 37.9 us
  Pallas kernels  37.2 us (98%)
  local copies, waits for them, and re-layouts  0.71 us (2%)
    pallas_call x1, Pallas kernels, body(): pl.pallas_call(functools.partial(kernel, n), out_shape=pltpu.VMEM((tokens...  37.2 us

profile of v7, /device:TPU:1, one launch (start us, length us, event | category | flops | bytes accessed | tf_op | source)
XLA Modules:
  0.0 37.9 jit_solution(7275809827683659980)
XLA Ops:
  0.0 37.2 %shard_map.127 = bf16[128,1024]{1,0:T(8,128)(2,1)S(1)} custom-call(bf16[128,512]{1,0:T(8,128)(2,1)} %q_hbm.1, bf16[128,512]{1,0:T(8,128)(2,1)} %k_hbm.1, bf16[128,512]{1,0:T(8,128)(2,1)} %v_hbm.1, f32[3,3,512]{2,1,0:T(4,128)} %taps_hbm.1, f32[128,512]{1,0:T(8,128)} %filter_hbm.1, f32[1,512]{1,0:T(1,128)} %bitcast.1, bf16[512,4096]{1,0:T(8,128)(2,1)} %weight_hbm.1, ...), custom_call_target="tpu_custom_call" | custom-call | tf_op jit(solution)/shard_map/pallas_call | solution.py:475
  37.2 0.7 %copy.15 = bf16[128,1024]{1,0:T(8,128)(2,1)} copy(bf16[128,1024]{1,0:T(8,128)(2,1)S(1)} %shard_map.127) | data formatting | bytes 524288

commit v8 on v7

--- a/solution.py
+++ b/solution.py
@@ -149,8 +149,6 @@
         *zip(parts_for(core), weight_slots(0)),
     ]
     loads = [pltpu.make_async_copy(src, dst, load_sem.at[i]) for i, (src, dst) in enumerate(pairs)]
-    for load in loads[:6]:
-        load.start()
 
     lines = ((2, 1), (2, 0), (1, 1), (3, 1), (1, 0), (3, 0), (0, 1), (0, 0))
 
@@ -172,6 +170,8 @@
         pl.semaphore_signal(barrier, inc=1, device_id=(peer, chan), device_id_type=MESH)
 
     rounds(greet)
+    for load in loads[:6]:
+        load.start()
     for neighbour in (other_core, *across):
         pl.semaphore_signal(barrier, inc=1, device_id=(me, neighbour), device_id_type=MESH)
     for load in loads[6:12]:

time: 38.1 us -> 38 us (level)
  no operation moved by 1% of the time
where the time goes in v8:
time: 38 us; the launch traced here: 37.9 us
  Pallas kernels  37.2 us (98%)
  local copies, waits for them, and re-layouts  0.71 us (2%)
    pallas_call x1, Pallas kernels, body(): pl.pallas_call(functools.partial(kernel, n), out_shape=pltpu.VMEM((tokens...  37.2 us

profile of v8, /device:TPU:1, one launch (start us, length us, event | category | flops | bytes accessed | tf_op | source)
XLA Modules:
  0.0 37.9 jit_solution(7183080504427985886)
XLA Ops:
  0.0 37.2 %shard_map.127 = bf16[128,1024]{1,0:T(8,128)(2,1)S(1)} custom-call(bf16[128,512]{1,0:T(8,128)(2,1)} %q_hbm.1, bf16[128,512]{1,0:T(8,128)(2,1)} %k_hbm.1, bf16[128,512]{1,0:T(8,128)(2,1)} %v_hbm.1, f32[3,3,512]{2,1,0:T(4,128)} %taps_hbm.1, f32[128,512]{1,0:T(8,128)} %filter_hbm.1, f32[1,512]{1,0:T(1,128)} %bitcast.1, bf16[512,4096]{1,0:T(8,128)(2,1)} %weight_hbm.1, ...), custom_call_target="tpu_custom_call" | custom-call | tf_op jit(solution)/shard_map/pallas_call | solution.py:475
  37.2 0.7 %copy.15 = bf16[128,1024]{1,0:T(8,128)(2,1)} copy(bf16[128,1024]{1,0:T(8,128)(2,1)S(1)} %shard_map.127) | data formatting | bytes 524288
